TPU v7x, 128 devices: a whole 4x4x4 slice. The times are simulated.
128 devices in a mesh: dp: 16 (over y_lo, x, core), ctx: 8 (over y_hi, z).
Axes of the slice: x: 4, y: 4 (y_hi: 2, y_lo: 2; y = y_hi * 2 + y_lo), z: 4, core: 2. Of those that a mesh axis runs over, the one named last changes fastest.
Arguments:
- tokens: bfloat16 [32, 1024, 4096], P('dp', 'ctx'), may hold values from -6 to 6
- queries: bfloat16 [32, 1024, 4096], P('dp', 'ctx'), may hold values from -6 to 6
- out_grad: bfloat16 [32, 1024, 4096], P('dp', 'ctx'), may hold values from -6 to 6
- kv_weight: bfloat16 [4096, 1024], replicated, may hold values from -0.09375 to 0.09375
- doc_lengths: int32 [32, 8], P('dp'), may hold values from 1 to 640, 1024 in all within a row
- swap_plan: int32 [16, 8, 3], P('dp', 'ctx'), may hold values from 0 to 1
Outputs:
- query_grad: bfloat16 [32, 1024, 4096], P('dp', 'ctx')
- weight_grad: float32 [4096, 1024], P(('dp', 'ctx'))
Inputs may be any that keep to these rules, and one draw needn't show every extreme that they name: `doc_lengths`: each row sums to 1024; its longest document has exactly 640 tokens. `swap_plan`: entry r names, among the device's pages (sequence first, then page order), the one traded in round r.
All inputs are finite; a program needn't handle non-finite values.
Results may differ from a plain program's by a relative error of at most 0.014.
Values may be sent and summed in bfloat16 or wider, within the bound.
No kernel may reach another device: no remote copies, remote signals or barrier semaphores. Data moves between devices by JAX's collectives and lax.ppermute only.
A program may use at most 256 MiB of HBM per device.

v0:
```python
import functools

import jax
import jax.numpy as jnp
from jax import lax
from jax.experimental import pallas as pl
from jax.experimental.pallas import tpu as pltpu
from jax.sharding import PartitionSpec as P

HEAD = 128
ROUNDS = 3
AXES = ("dp", "ctx")
N_DP = 16
N_CTX = 8
TEAM = 8
WINDOW = 6
BLOCK = 128
GROUPS = 4
CHUNKS = 2
SHARE = GROUPS // CHUNKS
VMEM = 48 * 1024 * 1024
MASKED = -1e30
JOIN = 6
LOG2E = 1.4426950408889634
NT = (((1,), (1,)), ((), ()))


def move(value, target):
    route = []
    for dp in range(N_DP):
        for ctx in range(N_CTX):
            to_dp, to_ctx = target(dp, ctx)
            if 0 <= to_ctx < N_CTX:
                route.append((dp * N_CTX + ctx, to_dp * N_CTX + to_ctx))
    return lax.ppermute(value, AXES, route)


def flip_dp(bits):
    return lambda dp, ctx: (dp ^ bits, ctx)


def flip_ctx(bits):
    return lambda dp, ctx: (dp, ctx ^ bits)


def shift_ctx(by):
    return lambda dp, ctx: (dp, ctx + by)


def shift_z(by, only=None, around=False):
    def target(dp, ctx):
        high, z = ctx // 4, ctx % 4
        if only is not None and (high, z) not in only:
            return dp, -1
        if not around and z + by > 3:
            return dp, -1
        return dp, high * 4 + (z + by) % 4

    return target


def lift(dp, ctx):
    return dp, ctx + 4


def flip_y(low, high):
    return lambda dp, ctx: (dp ^ (low * 8), ctx ^ (high * 4))


ANYWHERE = pl.BlockSpec(memory_space=pl.ANY)


def light(read):
    return dict(
        compiler_params=pltpu.CompilerParams(vmem_limit_bytes=VMEM),
        cost_estimate=pl.CostEstimate(flops=0, bytes_accessed=read, transcendentals=0),
    )


def copy_all(sems, pairs):
    copies = [
        pltpu.make_async_copy(source, target, sems.at[i])
        for i, (source, target) in enumerate(pairs)
    ]
    for copy in copies:
        copy.start()
    for copy in copies:
        copy.wait()


def copier(kernel, shapes, count, plan, *arrays):
    return pl.pallas_call(
        kernel,
        in_specs=[pl.BlockSpec(memory_space=pltpu.SMEM)] + [ANYWHERE] * len(arrays),
        out_specs=[pl.BlockSpec(memory_space=pltpu.VMEM)] * len(shapes),
        out_shape=[jax.ShapeDtypeStruct(shape, jnp.bfloat16) for shape in shapes],
        scratch_shapes=[pltpu.SemaphoreType.DMA((count,))],
        compiler_params=pltpu.CompilerParams(vmem_limit_bytes=VMEM),
        cost_estimate=pl.CostEstimate(flops=0, bytes_accessed=4 * 1024 * 1024, transcendentals=0),
    )(plan, *arrays)


def pages_of(plan, arrays, held_back=()):
    count = len(arrays)

    def kernel(plan_ref, *refs):
        outs, sems = refs[-1 - count : -1], refs[-1]
        copy_all(sems, [(ref.at[plan_ref[0]], out) for ref, out in zip(refs, outs)])

    return copier(kernel, [array.shape[1:] for array in arrays], count, plan, *arrays, *held_back)


def second_pages_of(plan, came, loaded, held_back=()):
    count = len(came)

    def kernel(plan_ref, *refs):
        out, sems = refs[-2], refs[-1]
        outs = [out.at[i] for i in range(count)]
        same = plan_ref[1] == plan_ref[0]

        @pl.when(same)
        def _():
            copy_all(sems, list(zip(refs[:count], outs)))

        @pl.when(jnp.logical_not(same))
        def _():
            others = [ref.at[1 - plan_ref[0]] for ref in refs[count : 2 * count]]
            copy_all(sems, list(zip(others, outs)))

    shape = (count,) + came[0].shape
    return copier(kernel, [shape], count, plan, *came, *loaded, *held_back)[0]


def third_pages_of(plan, came, came_before, loaded, part, parts, stays, held_back=()):
    count, toks, width = came.shape
    at = pl.ds(part * (width // parts), width // parts)
    whole = pl.ds(0, width)

    def kernel(plan_ref, came_ref, *refs):
        before, pages = refs[:count], refs[count : 2 * count]
        outs, sems = refs[-3 if stays else -2 : -1], refs[-1]
        first = plan_ref[1] == plan_ref[0]
        same = plan_ref[2] == plan_ref[1]

        def new(i, cols):
            return came_ref.at[i, :, cols]

        def old_from(came_first):
            def old(i, cols):
                if came_first:
                    return pages[i].at[1 - plan_ref[0], :, cols]
                return before[i].at[:, cols]

            return old

        for again in (True, False):
            for came_first in (True, False):

                @pl.when((same == again) & (first == came_first))
                def _():
                    old = old_from(came_first)
                    sources = (new, old) if again else (old, new)
                    pairs = [(sources[0](i, at), outs[0].at[i]) for i in range(count)]
                    if stays:
                        pairs += [(sources[1](i, whole), outs[1].at[i]) for i in range(count)]
                    copy_all(sems, pairs)

    shapes = [(count, toks, width // parts)] + [came.shape] * stays
    return copier(
        kernel, shapes, 2 * count, plan, came, *came_before, *loaded, *held_back
    )


def rows_of(plan, came, kept, held_back=()):
    def kernel(plan_ref, came_ref, kept_ref, *refs):
        out, sems = refs[-2:]
        slot = plan_ref[ROUNDS - 1]
        copy_all(sems, [(came_ref.at[0], out.at[slot]), (kept_ref.at[0], out.at[1 - slot])])

    return copier(kernel, [(2,) + came.shape[1:]], 2, plan, came, kept, *held_back)[0]


def sum_kernel(*refs):
    out_ref = refs[-1]
    half = out_ref.shape[-1] // 2
    for chunk in range(CHUNKS):
        parts = refs[chunk * WINDOW : (chunk + 1) * WINDOW]
        for group in range(SHARE):
            for kind in range(2):
                at = (group * 2 + kind) * HEAD
                to = kind * half + (chunk * SHARE + group) * HEAD
                total = parts[0][:, :, at : at + HEAD].astype(jnp.float32)
                for part in parts[1:]:
                    total = total + part[:, :, at : at + HEAD].astype(jnp.float32)
                out_ref[:, :, to : to + HEAD] = total.astype(out_ref.dtype)


def sum_of(chunks, held_back=()):
    vmem = pl.BlockSpec(memory_space=pltpu.VMEM)
    rows, toks, cols = chunks[0][0].shape
    return pl.pallas_call(
        sum_kernel,
        in_specs=[vmem] * (WINDOW * CHUNKS) + [ANYWHERE] * len(held_back),
        out_specs=vmem,
        out_shape=jax.ShapeDtypeStruct((rows, toks, cols * CHUNKS), jnp.bfloat16),
        **light(4 * 1024 * 1024),
    )(*[part for parts in chunks for part in parts], *held_back)


def columns_kernel(count, place_ref, *refs):
    sources, outs = refs[: 4 * count], refs[-count:]
    part = sources[0].shape[1]
    for k, out in enumerate(outs):
        for side in range(2):
            for low in range(2):
                out[side, :, low * part : (low + 1) * part] = sources[(k * 2 + side) * 2 + low][...]


def columns_of(place, flat, chips, held_back=()):
    rows, width = flat.shape
    part = width // (2 * TEAM)
    in_specs = []
    for k in chips:
        for side in range(2):
            for low in range(2):
                in_specs.append(
                    pl.BlockSpec(
                        (rows, part),
                        lambda i, p, bits=2 * k + side, low=low: (0, low * TEAM + (p[0] ^ bits)),
                    )
                )
    shape = jax.ShapeDtypeStruct((2, rows, 2 * part), flat.dtype)
    out = pl.BlockSpec((2, rows, 2 * part), lambda i, p: (0, 0, 0))
    return pl.pallas_call(
        functools.partial(columns_kernel, len(chips)),
        grid_spec=pltpu.PrefetchScalarGridSpec(
            num_scalar_prefetch=1,
            grid=(1,),
            in_specs=in_specs + [ANYWHERE] * len(held_back),
            out_specs=[out] * len(chips),
        ),
        out_shape=[shape] * len(chips),
        **light(1024 * 1024),
    )(place, *([flat] * len(in_specs)), *held_back)


def hold_kernel(*refs):
    pass


def hold(array, *held_back):
    return pl.pallas_call(
        hold_kernel,
        in_specs=[ANYWHERE] * (1 + len(held_back)),
        out_specs=ANYWHERE,
        out_shape=jax.ShapeDtypeStruct(array.shape, array.dtype),
        input_output_aliases={0: 0},
        **light(1024),
    )(array, *held_back)


def attention_kernel(info_ref, *refs):
    q_ref, d_ref = refs[:2]
    k_refs = refs[2 : 2 + WINDOW]
    v_refs = refs[2 + WINDOW : 2 + 2 * WINDOW]
    start_ref = refs[2 + 2 * WINDOW]
    outs = len(refs) - 7 - WINDOW
    dq_ref = refs[outs]
    part_refs = refs[outs + 1 : outs + 1 + WINDOW]
    q_s, d_s, w_s, dp_s, acc_s, sum_s = refs[-6:]
    first = info_ref[1]
    heads = q_ref.shape[-1] // HEAD
    scale = HEAD ** (-0.5)
    for head in range(heads):
        at = slice(head * HEAD, (head + 1) * HEAD)
        q_s[head * BLOCK : (head + 1) * BLOCK, :] = q_ref[0, :, at]
        d_s[head * BLOCK : (head + 1) * BLOCK, :] = d_ref[0, :, at]
    start = start_ref[0]
    key_iota = lax.broadcasted_iota(jnp.int32, (JOIN * BLOCK, BLOCK), 0)
    query_iota = lax.broadcasted_iota(jnp.int32, (JOIN * BLOCK, BLOCK), 1) + (WINDOW - 1) * BLOCK
    sum_s[...] = jnp.zeros_like(sum_s)
    acc_s[...] = jnp.zeros_like(acc_s)
    span = 2 * BLOCK
    spans = [slice(at, at + span) for at in range(0, heads * BLOCK, span)]

    def fold(array):
        return jnp.sum(array.reshape(JOIN * BLOCK // 8, 8, span), axis=0)

    for index in range(0, WINDOW, JOIN):
        at = slice(index * BLOCK, (index + JOIN) * BLOCK)

        @pl.when(index + JOIN > first)
        def _():
            key_pos = key_iota + index * BLOCK
            seen = (key_pos >= start) & (key_pos <= query_iota)
            bias = jnp.where(seen, 0.0, MASKED)
            bias = jnp.concatenate([bias, bias], axis=1)
            key = jnp.concatenate([k_refs[index + i][0] for i in range(JOIN)], axis=0)
            value = jnp.concatenate([v_refs[index + i][0] for i in range(JOIN)], axis=0)
            for cols in spans:
                scores = lax.dot_general(key, q_s[cols, :], NT, preferred_element_type=jnp.float32)
                dprobs = lax.dot_general(
                    value, d_s[cols, :], NT, preferred_element_type=jnp.float32
                )
                weights = jnp.exp2(scores * (scale * LOG2E) + bias)
                w_s[at, cols] = weights
                dp_s[at, cols] = dprobs
                sum_s[0:8, cols] += fold(weights)
                sum_s[8:16, cols] += fold(weights * dprobs)

    inverse = 1.0 / jnp.sum(sum_s[0:8, :], axis=0, keepdims=True)
    delta = jnp.sum(sum_s[8:16, :], axis=0, keepdims=True) * inverse

    for index in range(0, WINDOW, JOIN):
        at = slice(index * BLOCK, (index + JOIN) * BLOCK)
        joined = range(index, index + JOIN)

        @pl.when(index + JOIN <= first)
        def _():
            for i in joined:
                part_refs[i][0] = jnp.zeros(part_refs[i].shape[1:], jnp.bfloat16)

        @pl.when(index + JOIN > first)
        def _():
            key = [k_refs[i][0].astype(jnp.float32).T.astype(jnp.bfloat16) for i in joined]
            key = jnp.concatenate(key, axis=1)
            dk = jnp.zeros((JOIN * BLOCK, HEAD), jnp.float32)
            dv = jnp.zeros((JOIN * BLOCK, HEAD), jnp.float32)
            for cols in spans:
                probs = w_s[at, cols] * inverse[:, cols]
                dscores = (probs * (dp_s[at, cols] - delta[:, cols]) * scale).astype(jnp.bfloat16)
                dv += jnp.dot(
                    probs.astype(jnp.bfloat16), d_s[cols, :], preferred_element_type=jnp.float32
                )
                dk += jnp.dot(dscores, q_s[cols, :], preferred_element_type=jnp.float32)
                acc_s[:, cols] += jnp.dot(key, dscores, preferred_element_type=jnp.float32)
            for i in joined:
                rows = slice((i - index) * BLOCK, (i - index + 1) * BLOCK)
                part_refs[i][0, :, :HEAD] = dk[rows].astype(jnp.bfloat16)
                part_refs[i][0, :, HEAD:] = dv[rows].astype(jnp.bfloat16)

    for head in range(heads):
        at = slice(head * HEAD, (head + 1) * HEAD)
        dq_ref[0, :, at] = acc_s[:, head * BLOCK : (head + 1) * BLOCK].T.astype(jnp.bfloat16)


def attention(info, page, blocks, start, chunk, dq, parts, held_back=(), dq_width=4096):
    _, toks, page_width = page.shape
    rows = start.shape[0]
    width = dq_width // GROUPS
    first = chunk * SHARE if page_width == dq_width else 0
    queries = width // HEAD * toks
    pairs = SHARE * queries * WINDOW * BLOCK
    in_specs = [
        pl.BlockSpec((1, toks, width), lambda g, f: (0, 0, first + g)),
        pl.BlockSpec((1, toks, width), lambda g, f: (1, 0, first + g)),
    ]
    in_specs += [pl.BlockSpec((1, BLOCK, HEAD), lambda g, f: (f[0], 0, chunk * SHARE + g))] * WINDOW
    in_specs += [
        pl.BlockSpec((1, BLOCK, HEAD), lambda g, f: (f[0], 0, GROUPS + chunk * SHARE + g))
    ] * WINDOW
    in_specs += [pl.BlockSpec((1, 1, toks), lambda g, f: (f[0], 0, 0))]
    args = [page, page] + list(blocks) + list(blocks) + [start]
    aliases = {}
    for place, array in enumerate([dq] + list(parts)):
        if array is not None:
            aliases[1 + len(args)] = place
            in_specs.append(ANYWHERE)
            args.append(array)
    in_specs += [ANYWHERE] * len(held_back)
    args += held_back
    part_shape = jax.ShapeDtypeStruct((rows, BLOCK, SHARE * 2 * HEAD), jnp.bfloat16)
    spec = pltpu.PrefetchScalarGridSpec(
        num_scalar_prefetch=1,
        grid=(SHARE,),
        in_specs=in_specs,
        out_specs=[pl.BlockSpec((1, toks, width), lambda g, f: (f[0], 0, chunk * SHARE + g))]
        + [pl.BlockSpec((1, BLOCK, 2 * HEAD), lambda g, f: (f[0], 0, g))] * WINDOW,
        scratch_shapes=[
            pltpu.VMEM((queries, HEAD), jnp.bfloat16),
            pltpu.VMEM((queries, HEAD), jnp.bfloat16),
            pltpu.VMEM((WINDOW * BLOCK, queries), jnp.float32),
            pltpu.VMEM((WINDOW * BLOCK, queries), jnp.float32),
            pltpu.VMEM((HEAD, queries), jnp.float32),
            pltpu.VMEM((16, queries), jnp.float32),
        ],
    )
    return pl.pallas_call(
        attention_kernel,
        grid_spec=spec,
        out_shape=[jax.ShapeDtypeStruct((rows, toks, GROUPS * width), jnp.bfloat16)]
        + [part_shape] * WINDOW,
        input_output_aliases=aliases,
        compiler_params=pltpu.CompilerParams(vmem_limit_bytes=VMEM),
        cost_estimate=pl.CostEstimate(
            flops=10 * pairs * HEAD, bytes_accessed=4 * 1024 * 1024, transcendentals=pairs
        ),
    )(info, *args)


def arrange_kernel(plan_ref, place_ref, *refs):
    sources, out_ref = refs[:-1], refs[-1]
    rank_me, z_me, low_me, high_me = (place_ref[i] for i in range(4))
    for rel, source in enumerate(sources):
        for page in range(2):
            rank = rank_me ^ rel
            slot = jnp.int32(page)
            for step in range(ROUNDS):
                to_rank = rank ^ (1 << step)
                goes = plan_ref[(rank ^ rank_me) * ROUNDS + step] == slot
                slot = jnp.where(goes, plan_ref[(to_rank ^ rank_me) * ROUNDS + step], slot)
                rank = jnp.where(goes, to_rank, rank)
            column = pl.multiple_of(((rank ^ rank_me) * 2 + slot) * BLOCK, BLOCK)
            data = source[page * BLOCK : (page + 1) * BLOCK, :].astype(jnp.float32)
            data = data.T.astype(jnp.bfloat16)
            for low in range(2):
                for high in range(2):
                    for z in range(4):
                        at = ((low * 2 + high) * 4 + z) * 32
                        to = (z ^ z_me) * 4 + (low ^ low_me) + (high ^ high_me) * 2
                        to = pl.multiple_of(to * 32, 32)
                        out_ref[pl.ds(to, 32), pl.ds(column, BLOCK)] = data[at : at + 32, :]


def arrange(plan_all, place, sources):
    rows, cols = sources[0].shape
    return pl.pallas_call(
        arrange_kernel,
        grid_spec=pltpu.PrefetchScalarGridSpec(
            num_scalar_prefetch=2,
            grid=(1,),
            in_specs=[pl.BlockSpec((rows, cols), lambda i, a, b: (0, 0))] * len(sources),
            out_specs=pl.BlockSpec((cols, rows * len(sources)), lambda i, a, b: (0, 0)),
        ),
        out_shape=jax.ShapeDtypeStruct((cols, rows * len(sources)), jnp.bfloat16),
        compiler_params=pltpu.CompilerParams(vmem_limit_bytes=VMEM),
        cost_estimate=pl.CostEstimate(flops=0, bytes_accessed=4 * 1024 * 1024, transcendentals=0),
    )(plan_all, place, *sources)


def product_kernel(x_ref, *refs):
    grads, outs = refs[:TEAM], refs[TEAM:]
    for z, out in enumerate(outs):
        rows = slice(z * 4 * 32, (z + 1) * 4 * 32)
        total = None
        for rel, grad in enumerate(grads):
            span = 2 * BLOCK
            block = jnp.concatenate([grad[0], grad[1]], axis=0)
            term = jnp.dot(
                x_ref[rows, rel * span : (rel + 1) * span],
                block,
                preferred_element_type=jnp.float32,
            )
            total = term if total is None else total + term
        out[...] = total.astype(out.dtype)


def product(x, grads):
    cols = grads[0].shape[-1]
    shape = (x.shape[0] // 4, cols)
    return pl.pallas_call(
        product_kernel,
        out_shape=[jax.ShapeDtypeStruct(shape, jnp.float32)]
        + [jax.ShapeDtypeStruct(shape, jnp.bfloat16)] * 3,
        compiler_params=pltpu.CompilerParams(vmem_limit_bytes=VMEM),
        cost_estimate=pl.CostEstimate(
            flops=2 * x.shape[0] * x.shape[1] * cols,
            bytes_accessed=5 * 1024 * 1024,
            transcendentals=0,
        ),
    )(x, *grads)


def per_device(tokens, queries, out_grad, kv_weight, doc_lengths, swap_plan):
    seqs, toks, width = tokens.shape
    pair = kv_weight.shape[1]
    cols = pair // 2
    group_width = queries.shape[2] // GROUPS
    dp = lax.axis_index("dp")
    ctx = lax.axis_index("ctx")
    rank = lax.rem(dp, TEAM)
    z = lax.rem(ctx, 4)
    y_high = ctx // 4
    y_low = dp // TEAM
    plan = swap_plan[0, 0]
    plans = jnp.stack([plan] + [move(plan, flip_dp(2 * k)) for k in range(1, TEAM // 2)])
    plan_all = jnp.stack([plans, move(plans, flip_dp(1))], axis=1).reshape(-1)

    ends = jnp.cumsum(doc_lengths, axis=1)
    pos = ctx * toks + jnp.arange(toks, dtype=jnp.int32)
    begun = jnp.max(
        jnp.where(ends[:, None, :] <= pos[None, :, None], ends[:, None, :], 0), axis=2
    )
    start = begun - (ctx - (WINDOW - 1)) * toks
    first = jnp.clip(start[:, 0] // BLOCK, 0, WINDOW - 1)
    start = start[:, None, :]
    row_came = plan[ROUNDS - 1]
    row_kept = 1 - row_came
    info_came = jnp.stack([row_came, jnp.where(row_came == 0, first[0], first[1])])
    info_kept = jnp.stack([row_kept, jnp.where(row_kept == 0, first[0], first[1])])

    def cross(step, value):
        return move(value, flip_dp(1 << step))

    halves = [queries, out_grad]
    flat = tokens.reshape(seqs * toks, width)
    kv = jnp.dot(flat, kv_weight, preferred_element_type=jnp.float32).astype(jnp.bfloat16)
    kv = kv.reshape(seqs, toks, pair)
    kv_came = cross(0, pages_of(plan, [kv], [plan_all])[0])
    send = second_pages_of(plan, [kv_came], [kv])
    loaded = [cross(0, one) for one in pages_of(plan, halves, [send])]
    kv_second = cross(1, send)
    send, kv_kept = third_pages_of(plan, kv_second, [kv_came], [kv], 0, 1, True)
    kv_third = cross(2, send)
    send = second_pages_of(plan, loaded, halves)
    send = hold(send, kv_third)
    came = cross(1, send)
    own = rows_of(plan, kv_third, kv_kept, [send])
    near = [move(own, shift_z(by)) for by in (1, 2, 3)]
    above = move(own, lift)
    far = [
        move(above, shift_z(1, {(1, 0), (1, 1), (1, 2), (1, 3)}, True)),
        move(above, shift_z(2, {(1, 2), (1, 3)}, True)),
        move(above, shift_z(3, {(1, 1), (1, 2), (1, 3)}, True)),
    ]
    blocks = [
        far[0],
        above,
        near[2] + far[2],
        near[1] + far[1],
        jnp.where(z == 0, far[0], near[0]),
        own,
    ]
    send_a, kept = third_pages_of(
        plan, came, loaded, halves, 0, CHUNKS, True, held_back=near + far
    )
    came_a = cross(2, send_a)
    none = [None] * WINDOW

    def collect(parts):
        return parts[-1:] + [
            move(parts[WINDOW - 1 - by], shift_ctx(-by)) for by in range(1, WINDOW)
        ]

    there = [None] * (TEAM // 2)
    there[0], column = columns_of(rank[None], flat, [0, 2], [send_a])
    there[2] = move(column, flip_dp(4))
    dq, *parts_a = attention(info_kept, kept, blocks, start, 0, None, none)
    dq, *parts_b = attention(info_kept, kept, blocks, start, 1, dq, none)
    send_b = third_pages_of(
        plan, came, loaded, halves, 1, CHUNKS, False, held_back=[came_a, parts_b[0], there[2]]
    )[0]
    came_b = cross(2, send_b)
    dq, *parts_a = attention(info_came, came_a, blocks, start, 0, dq, parts_a)
    parts_a = collect(parts_a)
    columns = list(columns_of(rank[None], flat, [1, 3], [came_b]))
    for k, column in zip((1, 3), columns):
        there[k] = move(column, flip_dp(2 * k))
    dq, *parts_b = attention(
        info_came, came_b, blocks, start, 1, dq, parts_b, parts_a[1:4] + columns[:1]
    )
    grad = sum_of([parts_a, collect(parts_b)], [there[1], there[3]])

    sources = []
    for k in range(TEAM // 2):
        sources += [there[k][0], move(there[k][1], flip_dp(1))]
    place = jnp.stack([rank, z, y_low, y_high])
    arranged = arrange(plan_all, place, sources)
    grads = []
    for k in range(TEAM // 2):
        chip = move(grad, flip_dp(2 * k)) if k else grad
        grads += [chip, move(chip, flip_dp(1))]
    mine, *others = product(arranged, grads)
    for k, other in enumerate(others):
        mine = mine + move(other, flip_ctx(k + 1)).astype(jnp.float32)
    final = mine[:32]
    for k in range(1, 4):
        final = final + move(mine[32 * k : 32 * (k + 1)], flip_y(k % 2, k // 2))
    return dq, final


def solution(mesh):
    in_specs = (
        P("dp", "ctx", None),
        P("dp", "ctx", None),
        P("dp", "ctx", None),
        P(),
        P("dp", None),
        P("dp", "ctx", None),
    )
    out_specs = (P("dp", "ctx", None), P(("dp", "ctx"), None))
    return jax.shard_map(
        per_device, mesh=mesh, in_specs=in_specs, out_specs=out_specs, check_vma=False
    )
```

profile of v0, /device:TPU:0, one launch (start us, length us, event | category | flops | bytes accessed | tf_op | source)
XLA Modules:
  0.0 266.3 jit_solution(2046331903683021813)
XLA Ops:
  5.0 6.5 %convolution_convert_fusion = bf16[256,1024]{1,0:T(8,128)(2,1)S(1)} fusion(bf16[256,4096]{1,0:T(8,128)(2,1)} %bitcast.41, bf16[4096,1024]{1,0:T(8,128)(2,1)} %param.9), kind=kOutput, calls=%fused_computation | convolution fusion | flops 2147745792 | bytes 11010048 | tf_op jit(solution)/shard_map/dot_general | solution.py:507
  20.1 6.6 %collective-permute-done.7.came_ref = bf16[1,128,1024]{2,1,0:T(8,128)(2,1)S(1)} collective-permute-done((bf16[1,128,1024]{2,1,0:T(8,128)(2,1)S(1)}, bf16[1,128,1024]{2,1,0:T(8,128)(2,1)S(1)}, u32[]{:S(2)}, u32[]{:S(2)}) %collective-permute-start.7) | collective-permute-done | bytes 262176 | tf_op jit(solution)/shard_map/ppermute | solution.py:35
  32.8 4.0 %collective-permute-done.8.refs_1_.came_ref = bf16[1,128,1024]{2,1,0:T(8,128)(2,1)S(1)} collective-permute-done((bf16[1,128,1024]{2,1,0:T(8,128)(2,1)S(1)}, bf16[1,128,1024]{2,1,0:T(8,128)(2,1)S(1)}, u32[]{:S(2)}, u32[]{:S(2)}) %collective-permute-start.8) | collective-permute-done | bytes 262176 | tf_op jit(solution)/shard_map/ppermute | solution.py:35
  38.9 5.1 %collective-permute-start.13 = (bf16[2,128,1024]{2,1,0:T(8,128)(2,1)S(1)}, bf16[2,128,1024]{2,1,0:T(8,128)(2,1)S(1)}, u32[]{:S(2)}, u32[]{:S(2)}) collective-permute-start(bf16[2,128,1024]{2,1,0:T(8,128)(2,1)S(1)} %shard_map.83.refs_7_.refs_13_), channel_id=1, source_target_pairs={{0,4},{1,5},{2,6},{3,7},{8,12},{9,13},{10,14},{11,15},{16,20},{17,... | collective-permute-start | bytes 1572872 | tf_op jit(solution)/shard_map/ppermute | solution.py:35
  44.0 4.6 %collective-permute-start.10 = (bf16[2,128,1024]{2,1,0:T(8,128)(2,1)S(1)}, bf16[2,128,1024]{2,1,0:T(8,128)(2,1)}, u32[]{:S(2)}, u32[]{:S(2)}) collective-permute-start(bf16[2,128,1024]{2,1,0:T(8,128)(2,1)S(1)} %shard_map.83.refs_7_.refs_13_), channel_id=1, source_target_pairs={{0,1},{1,2},{2,3},{4,5},{5,6},{6,7},{8,9},{9,10},{10,11},{12,13},{... | collective-permute-start | bytes 1572872 | tf_op jit(solution)/shard_map/ppermute | solution.py:35
  48.7 4.7 %collective-permute-start.11 = (bf16[2,128,1024]{2,1,0:T(8,128)(2,1)S(1)}, bf16[2,128,1024]{2,1,0:T(8,128)(2,1)S(1)}, u32[]{:S(2)}, u32[]{:S(2)}) collective-permute-start(bf16[2,128,1024]{2,1,0:T(8,128)(2,1)S(1)} %shard_map.83.refs_7_.refs_13_), channel_id=1, source_target_pairs={{0,2},{1,3},{4,6},{5,7},{8,10},{9,11},{12,14},{13,15},{16,18},{17,... | collective-permute-start | bytes 1572872 | tf_op jit(solution)/shard_map/ppermute | solution.py:35
  60.9 7.4 %collective-permute-done.11.refs_5_ = bf16[2,128,1024]{2,1,0:T(8,128)(2,1)S(1)} collective-permute-done((bf16[2,128,1024]{2,1,0:T(8,128)(2,1)S(1)}, bf16[2,128,1024]{2,1,0:T(8,128)(2,1)S(1)}, u32[]{:S(2)}, u32[]{:S(2)}) %collective-permute-start.11) | collective-permute-done | bytes 524320 | tf_op jit(solution)/shard_map/ppermute | solution.py:35
  72.1 11.5 %collective-permute-done.9.came_ref = bf16[2,128,4096]{2,1,0:T(8,128)(2,1)} collective-permute-done((bf16[2,128,4096]{2,1,0:T(8,128)(2,1)}, bf16[2,128,4096]{2,1,0:T(8,128)(2,1)}, u32[]{:S(2)}, u32[]{:S(2)}) %collective-permute-start.9) | collective-permute-done | bytes 2097184 | tf_op jit(solution)/shard_map/ppermute | solution.py:35
  83.5 4.3 %shard_map.84 = (bf16[2,128,2048]{2,1,0:T(8,128)(2,1)}, bf16[2,128,4096]{2,1,0:T(8,128)(2,1)}) custom-call(s32[3]{0:T(128)S(1)} %bitcast.71, bf16[2,128,4096]{2,1,0:T(8,128)(2,1)} %collective-permute-done.9.came_ref, bf16[128,4096]{1,0:T(8,128)(2,1)S(1)} %collective-permute-done.5.refs_0_, bf16[128,4096]{1,0:T(8,128)(2,1)} %copy-done.15, ...), custom_call_target="tpu_custom_call" | custom-call | bytes 4194304 | tf_op jit(solution)/shard_map/pallas_call | solution.py:92
  97.4 7.6 %shard_map.85 = (bf16[2,128,4096]{2,1,0:T(8,128)(2,1)}, bf16[2,128,512]{2,1,0:T(8,128)(2,1)}, bf16[2,128,512]{2,1,0:T(8,128)(2,1)}, bf16[2,128,512]{2,1,0:T(8,12...) custom-call(s32[2]{0:T(128)S(1)} %pad_add_fusion.3.info_ref, ...), custom_call_target="tpu_custom_call" | custom-call | flops 2013265920 | bytes 4194304 | tf_op jit(solution)/shard_map/pallas_call | solution.py:388
  105.7 7.6 %shard_map.86 = (bf16[2,128,4096]{2,1,0:T(8,128)(2,1)}, bf16[2,128,512]{2,1,0:T(8,128)(2,1)S(1)}, bf16[2,128,512]{2,1,0:T(8,128)(2,1)S(1)}, bf16[2,128,512]{2,1,...) custom-call(s32[2]{0:T(128)S(1)} %pad_add_fusion.3.info_ref, ...), custom_call_target="tpu_custom_call", output_to_operand_aliasing={{0}: (16, {})} | custom-call | flops 2013265920 | bytes 4194304 | tf_op jit(solution)/shard_map/pallas_call | solution.py:388
  114.1 10.4 %collective-permute-done.18.refs_6_ = bf16[2,256,512]{2,1,0:T(8,128)(2,1)S(1)} collective-permute-done((bf16[2,256,512]{2,1,0:T(8,128)(2,1)S(1)}, bf16[2,256,512]{2,1,0:T(8,128)(2,1)S(1)}, u32[]{:S(2)}, u32[]{:S(2)}) %collective-permute-start.18) | collective-permute-done | bytes 524320 | tf_op jit(solution)/shard_map/ppermute | solution.py:35
  136.2 7.6 %shard_map.89 = (bf16[2,128,4096]{2,1,0:T(8,128)(2,1)}, bf16[2,128,512]{2,1,0:T(8,128)(2,1)}, bf16[2,128,512]{2,1,0:T(8,128)(2,1)}, bf16[2,128,512]{2,1,0:T(8,12...) custom-call(s32[2]{0:T(128)S(1)} %pad_add_fusion.2.info_ref, ...), custom_call_target="tpu_custom_call", output_to_operand_aliasing={{0}: (16, {}), {1}: (17, {}), {2}: (18, {}), {3}: (19, {}),... | custom-call | flops 2013265920 | bytes 4194304 | tf_op jit(solution)/shard_map/pallas_call | solution.py:388
  153.0 7.0 %collective-permute-done.21.refs_23_.refs_2_ = bf16[2,128,512]{2,1,0:T(8,128)(2,1)S(1)} collective-permute-done((bf16[2,128,512]{2,1,0:T(8,128)(2,1)}, bf16[2,128,512]{2,1,0:T(8,128)(2,1)S(1)}, u32[]{:S(2)}, u32[]{:S(2)}) %collective-permute-start.21) | collective-permute-done | bytes 262176 | tf_op jit(solution)/shard_map/ppermute | solution.py:35
  161.6 7.7 %shard_map.91 = (bf16[2,128,4096]{2,1,0:T(8,128)(2,1)}, bf16[2,128,512]{2,1,0:T(8,128)(2,1)S(1)}, bf16[2,128,512]{2,1,0:T(8,128)(2,1)S(1)}, bf16[2,128,512]{2,1,...) custom-call(s32[2]{0:T(128)S(1)} %pad_add_fusion.2.info_ref, ...), custom_call_target="tpu_custom_call", output_to_operand_aliasing={{0}: (16, {}), {1}: (17, {}), {2}: (18, {}), {3}: (19, {}),... | custom-call | flops 2013265920 | bytes 4194304 | tf_op jit(solution)/shard_map/pallas_call | solution.py:388
  177.4 8.9 %collective-permute-done.31.refs_7_ = bf16[2,128,512]{2,1,0:T(8,128)(2,1)S(1)} collective-permute-done((bf16[2,128,512]{2,1,0:T(8,128)(2,1)S(1)}, bf16[2,128,512]{2,1,0:T(8,128)(2,1)S(1)}, u32[]{:S(2)}, u32[]{:S(2)}) %collective-permute-start.31) | collective-permute-done | bytes 262176 | tf_op jit(solution)/shard_map/ppermute | solution.py:35
  187.6 5.6 %collective-permute-done.32.refs_8_ = bf16[2,128,512]{2,1,0:T(8,128)(2,1)S(1)} collective-permute-done((bf16[2,128,512]{2,1,0:T(8,128)(2,1)S(1)}, bf16[2,128,512]{2,1,0:T(8,128)(2,1)S(1)}, u32[]{:S(2)}, u32[]{:S(2)}) %collective-permute-start.32) | collective-permute-done | bytes 262176 | tf_op jit(solution)/shard_map/ppermute | solution.py:35
  195.9 5.5 %collective-permute-done.34.refs_10_ = bf16[2,128,512]{2,1,0:T(8,128)(2,1)S(1)} collective-permute-done((bf16[2,128,512]{2,1,0:T(8,128)(2,1)S(1)}, bf16[2,128,512]{2,1,0:T(8,128)(2,1)S(1)}, u32[]{:S(2)}, u32[]{:S(2)}) %collective-permute-start.34) | collective-permute-done | bytes 262176 | tf_op jit(solution)/shard_map/ppermute | solution.py:35
  201.4 4.3 %collective-permute-done.35.refs_11_ = bf16[2,128,512]{2,1,0:T(8,128)(2,1)S(1)} collective-permute-done((bf16[2,128,512]{2,1,0:T(8,128)(2,1)S(1)}, bf16[2,128,512]{2,1,0:T(8,128)(2,1)S(1)}, u32[]{:S(2)}, u32[]{:S(2)}) %collective-permute-start.35) | collective-permute-done | bytes 262176 | tf_op jit(solution)/shard_map/ppermute | solution.py:35
  213.2 6.9 %collective-permute-done.37.refs_2_ = bf16[2,128,1024]{2,1,0:T(8,128)(2,1)S(1)} collective-permute-done((bf16[2,128,1024]{2,1,0:T(8,128)(2,1)S(1)}, bf16[2,128,1024]{2,1,0:T(8,128)(2,1)S(1)}, u32[]{:S(2)}, u32[]{:S(2)}) %collective-permute-start.37) | collective-permute-done | bytes 524320 | tf_op jit(solution)/shard_map/ppermute | solution.py:35
  220.1 5.2 %collective-permute-done.39.refs_4_ = bf16[2,128,1024]{2,1,0:T(8,128)(2,1)} collective-permute-done((bf16[2,128,1024]{2,1,0:T(8,128)(2,1)S(1)}, bf16[2,128,1024]{2,1,0:T(8,128)(2,1)}, u32[]{:S(2)}, u32[]{:S(2)}) %collective-permute-start.39) | collective-permute-done | bytes 524320 | tf_op jit(solution)/shard_map/ppermute | solution.py:35
  233.2 4.8 %shard_map.94 = (f32[128,1024]{1,0:T(8,128)S(1)}, bf16[128,1024]{1,0:T(8,128)(2,1)S(1)}, bf16[128,1024]{1,0:T(8,128)(2,1)S(1)}, bf16[128,1024]{1,0:T(8,128)(2,1)S(1)}) custom-call(bf16[512,2048]{1,0:T(8,128)(2,1)} %copy-done.21, bf16[2,128,1024]{2,1,0:T(8,128)(2,1)S(1)} %shard_map.93.refs_0_, bf16[2,128,1024]{2,1,0:T(8,128)(2,1)} %collective-permute-done.36.refs_1_, ...), custom_call_target="tpu_custom_call" | custom-call | flops 2147483648 | bytes 5242880 | tf_op jit(solution)/shard_map/pallas_call | solution.py:461
  242.8 4.5 %collective-permute-done.43 = bf16[128,1024]{1,0:T(8,128)(2,1)S(1)} collective-permute-done((bf16[128,1024]{1,0:T(8,128)(2,1)S(1)}, bf16[128,1024]{1,0:T(8,128)(2,1)S(1)}, u32[]{:S(2)}, u32[]{:S(2)}) %collective-permute-start.43) | collective-permute-done | bytes 262176 | tf_op jit(solution)/shard_map/ppermute | solution.py:35
  247.2 6.0 %collective-permute-done.44 = bf16[128,1024]{1,0:T(8,128)(2,1)S(1)} collective-permute-done((bf16[128,1024]{1,0:T(8,128)(2,1)S(1)}, bf16[128,1024]{1,0:T(8,128)(2,1)S(1)}, u32[]{:S(2)}, u32[]{:S(2)}) %collective-permute-start.44) | collective-permute-done | bytes 262176 | tf_op jit(solution)/shard_map/ppermute | solution.py:35
  (202 shorter events, 106.8 us)
Async XLA Ops:
  36.9 46.6 %collective-permute-start.9 = (bf16[2,128,4096]{2,1,0:T(8,128)(2,1)}, bf16[2,128,4096]{2,1,0:T(8,128)(2,1)}, u32[]{:S(2)}, u32[]{:S(2)}) collective-permute-start(bf16[2,128,4096]{2,1,0:T(8,128)(2,1)} %shard_map.82.refs_0_), channel_id=1, source_target_pairs={{0,16},{1,17},{2,18},{3,19},{4,20},{5,21},{6,22},{7,23},{8,24},{9,... | collective-permute-start | bytes 6291464 | tf_op jit(solution)/shard_map/ppermute | solution.py:35
  38.9 18.0 %collective-permute-start.13 = (bf16[2,128,1024]{2,1,0:T(8,128)(2,1)S(1)}, bf16[2,128,1024]{2,1,0:T(8,128)(2,1)S(1)}, u32[]{:S(2)}, u32[]{:S(2)}) collective-permute-start(bf16[2,128,1024]{2,1,0:T(8,128)(2,1)S(1)} %shard_map.83.refs_7_.refs_13_), channel_id=1, source_target_pairs={{0,4},{1,5},{2,6},{3,7},{8,12},{9,13},{10,14},{11,15},{16,20},{17,... | collective-permute-start | bytes 1572872 | tf_op jit(solution)/shard_map/ppermute | solution.py:35
  44.0 16.2 %collective-permute-start.10 = (bf16[2,128,1024]{2,1,0:T(8,128)(2,1)S(1)}, bf16[2,128,1024]{2,1,0:T(8,128)(2,1)}, u32[]{:S(2)}, u32[]{:S(2)}) collective-permute-start(bf16[2,128,1024]{2,1,0:T(8,128)(2,1)S(1)} %shard_map.83.refs_7_.refs_13_), channel_id=1, source_target_pairs={{0,1},{1,2},{2,3},{4,5},{5,6},{6,7},{8,9},{9,10},{10,11},{12,13},{... | collective-permute-start | bytes 1572872 | tf_op jit(solution)/shard_map/ppermute | solution.py:35
  48.7 19.7 %collective-permute-start.11 = (bf16[2,128,1024]{2,1,0:T(8,128)(2,1)S(1)}, bf16[2,128,1024]{2,1,0:T(8,128)(2,1)S(1)}, u32[]{:S(2)}, u32[]{:S(2)}) collective-permute-start(bf16[2,128,1024]{2,1,0:T(8,128)(2,1)S(1)} %shard_map.83.refs_7_.refs_13_), channel_id=1, source_target_pairs={{0,2},{1,3},{4,6},{5,7},{8,10},{9,11},{12,14},{13,15},{16,18},{17,... | collective-permute-start | bytes 1572872 | tf_op jit(solution)/shard_map/ppermute | solution.py:35
  54.8 17.2 %collective-permute-start.12 = (bf16[2,128,1024]{2,1,0:T(8,128)(2,1)S(1)}, bf16[2,128,1024]{2,1,0:T(8,128)(2,1)S(1)}, u32[]{:S(2)}, u32[]{:S(2)}) collective-permute-start(bf16[2,128,1024]{2,1,0:T(8,128)(2,1)S(1)} %shard_map.83.refs_7_.refs_13_), channel_id=1, source_target_pairs={{0,3},{4,7},{8,11},{12,15},{16,19},{20,23},{24,27},{28,31},{32,35}... | collective-permute-start | bytes 1572872 | tf_op jit(solution)/shard_map/ppermute | solution.py:35
  56.9 15.1 %collective-permute-start.14 = (bf16[2,128,1024]{2,1,0:T(8,128)(2,1)S(1)}, bf16[2,128,1024]{2,1,0:T(8,128)(2,1)S(1)}, u32[]{:S(2)}, u32[]{:S(2)}) collective-permute-start(bf16[2,128,1024]{2,1,0:T(8,128)(2,1)S(1)} %collective-permute-done.13.refs_3_.refs_9_), channel_id=1, source_target_pairs={{4,5},{5,6},{6,7},{7,4},{12,13},{13,14},{14,15},{15,12},{20,21},{2... | collective-permute-start | bytes 1572872 | tf_op jit(solution)/shard_map/ppermute | solution.py:35
  88.6 35.9 %collective-permute-start.17 = (bf16[2,128,2048]{2,1,0:T(8,128)(2,1)}, bf16[2,128,2048]{2,1,0:T(8,128)(2,1)}, u32[]{:S(2)}, u32[]{:S(2)}) collective-permute-start(bf16[2,128,2048]{2,1,0:T(8,128)(2,1)} %get-tuple-element.48.refs_8_), channel_id=1, source_target_pairs={{0,32},{1,33},{2,34},{3,35},{4,36},{5,37},{6,38},{7,39},{8,40},{9,... | collective-permute-start | bytes 3145736 | tf_op jit(solution)/shard_map/ppermute | solution.py:35
  96.0 28.5 %collective-permute-start.18 = (bf16[2,256,512]{2,1,0:T(8,128)(2,1)S(1)}, bf16[2,256,512]{2,1,0:T(8,128)(2,1)S(1)}, u32[]{:S(2)}, u32[]{:S(2)}) collective-permute-start(bf16[2,256,512]{2,1,0:T(8,128)(2,1)S(1)} %get-tuple-element.52), channel_id=1, source_target_pairs={{0,32},{1,33},{2,34},{3,35},{4,36},{5,37},{6,38},{7,39},{8,40},{9,... | collective-permute-start | bytes 1572872 | tf_op jit(solution)/shard_map/ppermute | solution.py:35
  127.3 23.9 %collective-permute-start.19 = (bf16[2,128,2048]{2,1,0:T(8,128)(2,1)}, bf16[2,128,2048]{2,1,0:T(8,128)(2,1)}, u32[]{:S(2)}, u32[]{:S(2)}) collective-permute-start(bf16[2,128,2048]{2,1,0:T(8,128)(2,1)} %shard_map.88), channel_id=1, source_target_pairs={{0,32},{1,33},{2,34},{3,35},{4,36},{5,37},{6,38},{7,39},{8,40},{9,... | collective-permute-start | bytes 3145736 | tf_op jit(solution)/shard_map/ppermute | solution.py:35
  145.1 15.0 %collective-permute-start.21 = (bf16[2,128,512]{2,1,0:T(8,128)(2,1)}, bf16[2,128,512]{2,1,0:T(8,128)(2,1)S(1)}, u32[]{:S(2)}, u32[]{:S(2)}) collective-permute-start(bf16[2,128,512]{2,1,0:T(8,128)(2,1)} %get-tuple-element.67), channel_id=1, source_target_pairs={{2,0},{3,1},{4,2},{5,3},{6,4},{7,5},{10,8},{11,9},{12,10},{13,11},... | collective-permute-start | bytes 786440 | tf_op jit(solution)/shard_map/ppermute | solution.py:35
  146.4 15.1 %collective-permute-start.22 = (bf16[2,128,512]{2,1,0:T(8,128)(2,1)}, bf16[2,128,512]{2,1,0:T(8,128)(2,1)S(1)}, u32[]{:S(2)}, u32[]{:S(2)}) collective-permute-start(bf16[2,128,512]{2,1,0:T(8,128)(2,1)} %get-tuple-element.68), channel_id=1, source_target_pairs={{3,0},{4,1},{5,2},{6,3},{7,4},{11,8},{12,9},{13,10},{14,11},{15,12... | collective-permute-start | bytes 786440 | tf_op jit(solution)/shard_map/ppermute | solution.py:35
  147.7 26.0 %collective-permute-start.29 = (bf16[2,128,512]{2,1,0:T(8,128)(2,1)}, bf16[2,128,512]{2,1,0:T(8,128)(2,1)S(1)}, u32[]{:S(2)}, u32[]{:S(2)}) collective-permute-start(bf16[2,128,512]{2,1,0:T(8,128)(2,1)} %get-tuple-element.74), channel_id=1, source_target_pairs={{4,0},{5,1},{6,2},{7,3},{12,8},{13,9},{14,10},{15,11},{20,16},{21,... | collective-permute-start | bytes 786440 | tf_op jit(solution)/shard_map/ppermute | solution.py:35
  151.2 24.9 %collective-permute-start.30 = (bf16[2,128,512]{2,1,0:T(8,128)(2,1)}, bf16[2,128,512]{2,1,0:T(8,128)(2,1)S(1)}, u32[]{:S(2)}, u32[]{:S(2)}) collective-permute-start(bf16[2,128,512]{2,1,0:T(8,128)(2,1)} %get-tuple-element.75), channel_id=1, source_target_pairs={{5,0},{6,1},{7,2},{13,8},{14,9},{15,10},{21,16},{22,17},{23,18},{2... | collective-permute-start | bytes 786440 | tf_op jit(solution)/shard_map/ppermute | solution.py:35
  169.3 17.0 %collective-permute-start.31 = (bf16[2,128,512]{2,1,0:T(8,128)(2,1)S(1)}, bf16[2,128,512]{2,1,0:T(8,128)(2,1)S(1)}, u32[]{:S(2)}, u32[]{:S(2)}) collective-permute-start(bf16[2,128,512]{2,1,0:T(8,128)(2,1)S(1)} %get-tuple-element.77), channel_id=1, source_target_pairs={{1,0},{2,1},{3,2},{4,3},{5,4},{6,5},{7,6},{9,8},{10,9},{11,10},{12... | collective-permute-start | bytes 786440 | tf_op jit(solution)/shard_map/ppermute | solution.py:35
  170.6 22.6 %collective-permute-start.32 = (bf16[2,128,512]{2,1,0:T(8,128)(2,1)S(1)}, bf16[2,128,512]{2,1,0:T(8,128)(2,1)S(1)}, u32[]{:S(2)}, u32[]{:S(2)}) collective-permute-start(bf16[2,128,512]{2,1,0:T(8,128)(2,1)S(1)} %get-tuple-element.78), channel_id=1, source_target_pairs={{2,0},{3,1},{4,2},{5,3},{6,4},{7,5},{10,8},{11,9},{12,10},{13,11},... | collective-permute-start | bytes 786440 | tf_op jit(solution)/shard_map/ppermute | solution.py:35
  171.9 33.8 %collective-permute-start.24 = (bf16[2,256,512]{2,1,0:T(8,128)(2,1)S(1)}, bf16[2,256,512]{2,1,0:T(8,128)(2,1)S(1)}, u32[]{:S(2)}, u32[]{:S(2)}) collective-permute-start(bf16[2,256,512]{2,1,0:T(8,128)(2,1)S(1)} %get-tuple-element.69.refs_25_), channel_id=1, source_target_pairs={{0,16},{1,17},{2,18},{3,19},{4,20},{5,21},{6,22},{7,23},{8,24},{9,... | collective-permute-start | bytes 1572872 | tf_op jit(solution)/shard_map/ppermute | solution.py:35
  173.7 32.0 %collective-permute-start.27 = (bf16[2,256,512]{2,1,0:T(8,128)(2,1)S(1)}, bf16[2,256,512]{2,1,0:T(8,128)(2,1)S(1)}, u32[]{:S(2)}, u32[]{:S(2)}) collective-permute-start(bf16[2,256,512]{2,1,0:T(8,128)(2,1)S(1)} %get-tuple-element.72), channel_id=1, source_target_pairs={{0,48},{1,49},{2,50},{3,51},{4,52},{5,53},{6,54},{7,55},{8,56},{9,... | collective-permute-start | bytes 1572872 | tf_op jit(solution)/shard_map/ppermute | solution.py:35
  176.1 19.8 %collective-permute-start.33 = (bf16[2,128,512]{2,1,0:T(8,128)(2,1)S(1)}, bf16[2,128,512]{2,1,0:T(8,128)(2,1)S(1)}, u32[]{:S(2)}, u32[]{:S(2)}) collective-permute-start(bf16[2,128,512]{2,1,0:T(8,128)(2,1)S(1)} %get-tuple-element.79), channel_id=1, source_target_pairs={{3,0},{4,1},{5,2},{6,3},{7,4},{11,8},{12,9},{13,10},{14,11},{15,12... | collective-permute-start | bytes 786440 | tf_op jit(solution)/shard_map/ppermute | solution.py:35
  186.3 15.1 %collective-permute-start.34 = (bf16[2,128,512]{2,1,0:T(8,128)(2,1)S(1)}, bf16[2,128,512]{2,1,0:T(8,128)(2,1)S(1)}, u32[]{:S(2)}, u32[]{:S(2)}) collective-permute-start(bf16[2,128,512]{2,1,0:T(8,128)(2,1)S(1)} %get-tuple-element.80), channel_id=1, source_target_pairs={{4,0},{5,1},{6,2},{7,3},{12,8},{13,9},{14,10},{15,11},{20,16},{21,... | collective-permute-start | bytes 786440 | tf_op jit(solution)/shard_map/ppermute | solution.py:35
  206.2 19.0 %collective-permute-start.39 = (bf16[2,128,1024]{2,1,0:T(8,128)(2,1)S(1)}, bf16[2,128,1024]{2,1,0:T(8,128)(2,1)}, u32[]{:S(2)}, u32[]{:S(2)}) collective-permute-start(bf16[2,128,1024]{2,1,0:T(8,128)(2,1)S(1)} %shard_map.93.refs_0_), channel_id=1, source_target_pairs={{0,32},{1,33},{2,34},{3,35},{4,36},{5,37},{6,38},{7,39},{8,40},{9,... | collective-permute-start | bytes 1572872 | tf_op jit(solution)/shard_map/ppermute | solution.py:35
  208.1 20.0 %collective-permute-start.41 = (bf16[2,128,1024]{2,1,0:T(8,128)(2,1)S(1)}, bf16[2,128,1024]{2,1,0:T(8,128)(2,1)}, u32[]{:S(2)}, u32[]{:S(2)}) collective-permute-start(bf16[2,128,1024]{2,1,0:T(8,128)(2,1)S(1)} %shard_map.93.refs_0_), channel_id=1, source_target_pairs={{0,48},{1,49},{2,50},{3,51},{4,52},{5,53},{6,54},{7,55},{8,56},{9,... | collective-permute-start | bytes 1572872 | tf_op jit(solution)/shard_map/ppermute | solution.py:35
  212.6 15.6 %collective-permute-start.25 = (bf16[256,512]{1,0:T(8,128)(2,1)S(1)}, bf16[256,512]{1,0:T(8,128)(2,1)S(1)}, u32[]{:S(2)}, u32[]{:S(2)}) collective-permute-start(bf16[256,512]{1,0:T(8,128)(2,1)S(1)} %get-tuple-element.93), channel_id=1, source_target_pairs={{0,8},{1,9},{2,10},{3,11},{4,12},{5,13},{6,14},{7,15},{8,0},{9,1},... | collective-permute-start | bytes 786440 | tf_op jit(solution)/shard_map/ppermute | solution.py:35
  213.0 20.2 %collective-permute-start.36 = (bf16[2,128,1024]{2,1,0:T(8,128)(2,1)S(1)}, bf16[2,128,1024]{2,1,0:T(8,128)(2,1)}, u32[]{:S(2)}, u32[]{:S(2)}) collective-permute-start(bf16[2,128,1024]{2,1,0:T(8,128)(2,1)S(1)} %shard_map.93.refs_0_), channel_id=1, source_target_pairs={{0,8},{1,9},{2,10},{3,11},{4,12},{5,13},{6,14},{7,15},{8,0},{9,1},... | collective-permute-start | bytes 1572872 | tf_op jit(solution)/shard_map/ppermute | solution.py:35
  238.1 15.2 %collective-permute-start.44 = (bf16[128,1024]{1,0:T(8,128)(2,1)S(1)}, bf16[128,1024]{1,0:T(8,128)(2,1)S(1)}, u32[]{:S(2)}, u32[]{:S(2)}) collective-permute-start(bf16[128,1024]{1,0:T(8,128)(2,1)S(1)} %get-tuple-element.84), channel_id=1, source_target_pairs={{0,2},{1,3},{2,0},{3,1},{4,6},{5,7},{6,4},{7,5},{8,10},{9,11},{10,... | collective-permute-start | bytes 786440 | tf_op jit(solution)/shard_map/ppermute | solution.py:35
  (67 other events, 595.7 us)
where the time goes:
time: 267 us; the launch traced here: 266 us
  waiting for transfers between devices  121 us (45%)
  starting transfers between devices  66.2 us (25%)
  Pallas kernels  50.7 us (19%)
  local copies, waits for them, and re-layouts  11.8 us (4%)
  matrix products  6.49 us (2%)
  between operations  5.13 us (2%)
  other arithmetic  4.84 us (2%)
    ppermute x49, waiting for transfers between devices, move(): return lax.ppermute(value, AXES, route)  121 us
    ppermute x49, starting transfers between devices, move(): return lax.ppermute(value, AXES, route)  66.2 us
    pallas_call x4, Pallas kernels, attention(): pl.pallas_call(attention_kernel, grid_spec=spec, out_shape=[jax.ShapeDtyp...  30.5 us
    pallas_call x8, Pallas kernels, copier(): pl.pallas_call(kernel, in_specs=[pl.BlockSpec(memory_space=pltpu.SMEM)] +...  13.3 us
    unnamed x84, local copies, waits for them, and re-layouts  10.3 us
    dot_general x1, matrix products, per_device(): jnp.dot(flat, kv_weight, preferred_element_type=jnp.float32)  6.49 us
  transfers between devices with their start and end apart: 49, of which 31 were waited for; matrix products, arithmetic and copies ran while one was open for 4% of the time, Pallas kernels for 13%

commit v1 on v0

--- a/solution.py
+++ b/solution.py
@@ -559,13 +559,13 @@
     dq, *parts_b = attention(
         info_came, came_b, blocks, start, 1, dq, parts_b, parts_a[1:4] + columns[:1]
     )
-    grad = sum_of([parts_a, collect(parts_b)], [there[1], there[3]])
-
     sources = []
     for k in range(TEAM // 2):
         sources += [there[k][0], move(there[k][1], flip_dp(1))]
     place = jnp.stack([rank, z, y_low, y_high])
     arranged = arrange(plan_all, place, sources)
+    grad = sum_of([parts_a, collect(parts_b)], [arranged])
+
     grads = []
     for k in range(TEAM // 2):
         chip = move(grad, flip_dp(2 * k)) if k else grad

time: 267 us -> 301 us (1.13)
  waiting for transfers between devices: 121 us -> 144 us
  local copies, waits for them, and re-layouts: 11.8 us -> 18 us
    ppermute x49, waiting for transfers between devices: 121 us -> 144 us  [move(): return lax.ppermute(value, AXES, route)]
    unnamed x84 -> x112, local copies, waits for them, and re-layouts: 10.3 us -> 15.7 us
  transfers between devices with their start and end apart: 49 -> 49, of which waited for: 31 -> 30; matrix products, arithmetic and copies ran while one was open for 4% -> 4% of each run, Pallas kernels for 13% -> 12%
where the time goes in v1:
time: 301 us; the launch traced here: 298 us
  waiting for transfers between devices  144 us (48%)
  starting transfers between devices  68.3 us (23%)
  Pallas kernels  50.8 us (17%)
  local copies, waits for them, and re-layouts  18 us (6%)
  matrix products  6.49 us (2%)
  between operations  5.34 us (2%)
  other arithmetic  4.84 us (2%)
    ppermute x49, waiting for transfers between devices, move(): return lax.ppermute(value, AXES, route)  144 us
    ppermute x49, starting transfers between devices, move(): return lax.ppermute(value, AXES, route)  68.3 us
    pallas_call x4, Pallas kernels, attention(): pl.pallas_call(attention_kernel, grid_spec=spec, out_shape=[jax.ShapeDtyp...  30.7 us
    unnamed x112, local copies, waits for them, and re-layouts  15.7 us
    pallas_call x8, Pallas kernels, copier(): pl.pallas_call(kernel, in_specs=[pl.BlockSpec(memory_space=pltpu.SMEM)] +...  13.2 us
    dot_general x1, matrix products, per_device(): jnp.dot(flat, kv_weight, preferred_element_type=jnp.float32)  6.49 us
  transfers between devices with their start and end apart: 49, of which 30 were waited for; matrix products, arithmetic and copies ran while one was open for 4% of the time, Pallas kernels for 12%

profile of v1, /device:TPU:0, one launch (start us, length us, event | category | flops | bytes accessed | tf_op | source)
XLA Modules:
  0.0 298.0 jit_solution(9495038179928683929)
XLA Ops:
  5.0 6.5 %convolution_convert_fusion = bf16[256,1024]{1,0:T(8,128)(2,1)S(1)} fusion(bf16[256,4096]{1,0:T(8,128)(2,1)} %bitcast.41, bf16[4096,1024]{1,0:T(8,128)(2,1)} %param.9), kind=kOutput, calls=%fused_computation | convolution fusion | flops 2147745792 | bytes 11010048 | tf_op jit(solution)/shard_map/dot_general | solution.py:507
  20.1 6.6 %collective-permute-done.7.came_ref = bf16[1,128,1024]{2,1,0:T(8,128)(2,1)S(1)} collective-permute-done((bf16[1,128,1024]{2,1,0:T(8,128)(2,1)S(1)}, bf16[1,128,1024]{2,1,0:T(8,128)(2,1)S(1)}, u32[]{:S(2)}, u32[]{:S(2)}) %collective-permute-start.7) | collective-permute-done | bytes 262176 | tf_op jit(solution)/shard_map/ppermute | solution.py:35
  38.9 5.1 %collective-permute-start.13 = (bf16[2,128,1024]{2,1,0:T(8,128)(2,1)S(1)}, bf16[2,128,1024]{2,1,0:T(8,128)(2,1)S(1)}, u32[]{:S(2)}, u32[]{:S(2)}) collective-permute-start(bf16[2,128,1024]{2,1,0:T(8,128)(2,1)S(1)} %shard_map.83.refs_7_.refs_13_), channel_id=1, source_target_pairs={{0,4},{1,5},{2,6},{3,7},{8,12},{9,13},{10,14},{11,15},{16,20},{17,... | collective-permute-start | bytes 1572872 | tf_op jit(solution)/shard_map/ppermute | solution.py:35
  44.0 4.6 %collective-permute-start.10 = (bf16[2,128,1024]{2,1,0:T(8,128)(2,1)S(1)}, bf16[2,128,1024]{2,1,0:T(8,128)(2,1)}, u32[]{:S(2)}, u32[]{:S(2)}) collective-permute-start(bf16[2,128,1024]{2,1,0:T(8,128)(2,1)S(1)} %shard_map.83.refs_7_.refs_13_), channel_id=1, source_target_pairs={{0,1},{1,2},{2,3},{4,5},{5,6},{6,7},{8,9},{9,10},{10,11},{12,13},{... | collective-permute-start | bytes 1572872 | tf_op jit(solution)/shard_map/ppermute | solution.py:35
  48.7 4.7 %collective-permute-start.11 = (bf16[2,128,1024]{2,1,0:T(8,128)(2,1)S(1)}, bf16[2,128,1024]{2,1,0:T(8,128)(2,1)S(1)}, u32[]{:S(2)}, u32[]{:S(2)}) collective-permute-start(bf16[2,128,1024]{2,1,0:T(8,128)(2,1)S(1)} %shard_map.83.refs_7_.refs_13_), channel_id=1, source_target_pairs={{0,2},{1,3},{4,6},{5,7},{8,10},{9,11},{12,14},{13,15},{16,18},{17,... | collective-permute-start | bytes 1572872 | tf_op jit(solution)/shard_map/ppermute | solution.py:35
  60.9 7.4 %collective-permute-done.11.refs_5_ = bf16[2,128,1024]{2,1,0:T(8,128)(2,1)S(1)} collective-permute-done((bf16[2,128,1024]{2,1,0:T(8,128)(2,1)S(1)}, bf16[2,128,1024]{2,1,0:T(8,128)(2,1)S(1)}, u32[]{:S(2)}, u32[]{:S(2)}) %collective-permute-start.11) | collective-permute-done | bytes 524320 | tf_op jit(solution)/shard_map/ppermute | solution.py:35
  72.1 11.4 %collective-permute-done.9.came_ref = bf16[2,128,4096]{2,1,0:T(8,128)(2,1)} collective-permute-done((bf16[2,128,4096]{2,1,0:T(8,128)(2,1)}, bf16[2,128,4096]{2,1,0:T(8,128)(2,1)}, u32[]{:S(2)}, u32[]{:S(2)}) %collective-permute-start.9) | collective-permute-done | bytes 2097184 | tf_op jit(solution)/shard_map/ppermute | solution.py:35
  83.5 4.1 %shard_map.84 = (bf16[2,128,2048]{2,1,0:T(8,128)(2,1)}, bf16[2,128,4096]{2,1,0:T(8,128)(2,1)}) custom-call(s32[3]{0:T(128)S(1)} %bitcast.71, bf16[2,128,4096]{2,1,0:T(8,128)(2,1)} %collective-permute-done.9.came_ref, bf16[128,4096]{1,0:T(8,128)(2,1)S(1)} %collective-permute-done.5.refs_0_, bf16[128,4096]{1,0:T(8,128)(2,1)} %copy-done.14, ...), custom_call_target="tpu_custom_call" | custom-call | bytes 4194304 | tf_op jit(solution)/shard_map/pallas_call | solution.py:92
  97.3 7.6 %shard_map.85 = (bf16[2,128,4096]{2,1,0:T(8,128)(2,1)}, bf16[2,128,512]{2,1,0:T(8,128)(2,1)S(1)}, bf16[2,128,512]{2,1,0:T(8,128)(2,1)S(1)}, bf16[2,128,512]{2,1,...) custom-call(s32[2]{0:T(128)S(1)} %pad_add_fusion.3.info_ref, ...), custom_call_target="tpu_custom_call" | custom-call | flops 2013265920 | bytes 4194304 | tf_op jit(solution)/shard_map/pallas_call | solution.py:388
  109.2 7.7 %shard_map.86 = (bf16[2,128,4096]{2,1,0:T(8,128)(2,1)}, bf16[2,128,512]{2,1,0:T(8,128)(2,1)S(1)}, bf16[2,128,512]{2,1,0:T(8,128)(2,1)}, bf16[2,128,512]{2,1,0:T(...) custom-call(s32[2]{0:T(128)S(1)} %pad_add_fusion.3.info_ref, ...), custom_call_target="tpu_custom_call", output_to_operand_aliasing={{0}: (16, {})} | custom-call | flops 2013265920 | bytes 4194304 | tf_op jit(solution)/shard_map/pallas_call | solution.py:388
  116.9 7.3 %collective-permute-done.18.refs_6_ = bf16[2,256,512]{2,1,0:T(8,128)(2,1)S(1)} collective-permute-done((bf16[2,256,512]{2,1,0:T(8,128)(2,1)S(1)}, bf16[2,256,512]{2,1,0:T(8,128)(2,1)S(1)}, u32[]{:S(2)}, u32[]{:S(2)}) %collective-permute-start.18) | collective-permute-done | bytes 524320 | tf_op jit(solution)/shard_map/ppermute | solution.py:35
  132.1 18.8 %collective-permute-done.19.refs_8_.refs_0_.refs_1_ = bf16[2,128,2048]{2,1,0:T(8,128)(2,1)} collective-permute-done((bf16[2,128,2048]{2,1,0:T(8,128)(2,1)}, bf16[2,128,2048]{2,1,0:T(8,128)(2,1)}, u32[]{:S(2)}, u32[]{:S(2)}) %collective-permute-start.19) | collective-permute-done | bytes 1048608 | tf_op jit(solution)/shard_map/ppermute | solution.py:35
  156.1 7.7 %shard_map.89 = (bf16[2,128,4096]{2,1,0:T(8,128)(2,1)}, bf16[2,128,512]{2,1,0:T(8,128)(2,1)S(1)}, bf16[2,128,512]{2,1,0:T(8,128)(2,1)S(1)}, bf16[2,128,512]{2,1,...) custom-call(s32[2]{0:T(128)S(1)} %pad_add_fusion.2.info_ref, ...), custom_call_target="tpu_custom_call", output_to_operand_aliasing={{0}: (16, {}), {1}: (17, {}), {2}: (18, {}), {3}: (19, {}),... | custom-call | flops 2013265920 | bytes 4194304 | tf_op jit(solution)/shard_map/pallas_call | solution.py:388
  177.1 5.5 %collective-permute-done.22.refs_24_.refs_3_ = bf16[2,128,512]{2,1,0:T(8,128)(2,1)S(1)} collective-permute-done((bf16[2,128,512]{2,1,0:T(8,128)(2,1)S(1)}, bf16[2,128,512]{2,1,0:T(8,128)(2,1)S(1)}, u32[]{:S(2)}, u32[]{:S(2)}) %collective-permute-start.22) | collective-permute-done | bytes 262176 | tf_op jit(solution)/shard_map/ppermute | solution.py:35
  182.6 7.7 %shard_map.91 = (bf16[2,128,4096]{2,1,0:T(8,128)(2,1)}, bf16[2,128,512]{2,1,0:T(8,128)(2,1)S(1)}, bf16[2,128,512]{2,1,0:T(8,128)(2,1)}, bf16[2,128,512]{2,1,0:T(...) custom-call(s32[2]{0:T(128)S(1)} %pad_add_fusion.2.info_ref, ...), custom_call_target="tpu_custom_call", output_to_operand_aliasing={{0}: (16, {}), {1}: (17, {}), {2}: (18, {}), {3}: (19, {}),... | custom-call | flops 2013265920 | bytes 4194304 | tf_op jit(solution)/shard_map/pallas_call | solution.py:388
  192.3 5.8 %collective-permute-done.29.refs_4_ = bf16[2,128,512]{2,1,0:T(8,128)(2,1)S(1)} collective-permute-done((bf16[2,128,512]{2,1,0:T(8,128)(2,1)S(1)}, bf16[2,128,512]{2,1,0:T(8,128)(2,1)S(1)}, u32[]{:S(2)}, u32[]{:S(2)}) %collective-permute-start.29) | collective-permute-done | bytes 262176 | tf_op jit(solution)/shard_map/ppermute | solution.py:35
  217.2 5.0 %collective-permute-done.33.refs_9_ = bf16[2,128,512]{2,1,0:T(8,128)(2,1)S(1)} collective-permute-done((bf16[2,128,512]{2,1,0:T(8,128)(2,1)}, bf16[2,128,512]{2,1,0:T(8,128)(2,1)S(1)}, u32[]{:S(2)}, u32[]{:S(2)}) %collective-permute-start.33) | collective-permute-done | bytes 262176 | tf_op jit(solution)/shard_map/ppermute | solution.py:35
  222.3 9.3 %collective-permute-done.34.refs_10_ = bf16[2,128,512]{2,1,0:T(8,128)(2,1)S(1)} collective-permute-done((bf16[2,128,512]{2,1,0:T(8,128)(2,1)}, bf16[2,128,512]{2,1,0:T(8,128)(2,1)S(1)}, u32[]{:S(2)}, u32[]{:S(2)}) %collective-permute-start.34) | collective-permute-done | bytes 262176 | tf_op jit(solution)/shard_map/ppermute | solution.py:35
  231.5 5.2 %collective-permute-done.35.refs_11_ = bf16[2,128,512]{2,1,0:T(8,128)(2,1)} collective-permute-done((bf16[2,128,512]{2,1,0:T(8,128)(2,1)S(1)}, bf16[2,128,512]{2,1,0:T(8,128)(2,1)}, u32[]{:S(2)}, u32[]{:S(2)}) %collective-permute-start.35) | collective-permute-done | bytes 262176 | tf_op jit(solution)/shard_map/ppermute | solution.py:35
  242.9 10.2 %collective-permute-done.37.refs_2_ = bf16[2,128,1024]{2,1,0:T(8,128)(2,1)S(1)} collective-permute-done((bf16[2,128,1024]{2,1,0:T(8,128)(2,1)S(1)}, bf16[2,128,1024]{2,1,0:T(8,128)(2,1)S(1)}, u32[]{:S(2)}, u32[]{:S(2)}) %collective-permute-start.37) | collective-permute-done | bytes 524320 | tf_op jit(solution)/shard_map/ppermute | solution.py:35
  253.1 10.0 %collective-permute-done.39.refs_4_ = bf16[2,128,1024]{2,1,0:T(8,128)(2,1)S(1)} collective-permute-done((bf16[2,128,1024]{2,1,0:T(8,128)(2,1)S(1)}, bf16[2,128,1024]{2,1,0:T(8,128)(2,1)S(1)}, u32[]{:S(2)}, u32[]{:S(2)}) %collective-permute-start.39) | collective-permute-done | bytes 524320 | tf_op jit(solution)/shard_map/ppermute | solution.py:35
  271.8 4.6 %collective-permute-start.45 = (bf16[128,1024]{1,0:T(8,128)(2,1)S(1)}, bf16[128,1024]{1,0:T(8,128)(2,1)S(1)}, u32[]{:S(2)}, u32[]{:S(2)}) collective-permute-start(bf16[128,1024]{1,0:T(8,128)(2,1)S(1)} %get-tuple-element.85), channel_id=1, source_target_pairs={{0,3},{1,2},{2,1},{3,0},{4,7},{5,6},{6,5},{7,4},{8,11},{9,10},{10,... | collective-permute-start | bytes 786440 | tf_op jit(solution)/shard_map/ppermute | solution.py:35
  276.4 4.5 %collective-permute-done.43 = bf16[128,1024]{1,0:T(8,128)(2,1)S(1)} collective-permute-done((bf16[128,1024]{1,0:T(8,128)(2,1)S(1)}, bf16[128,1024]{1,0:T(8,128)(2,1)S(1)}, u32[]{:S(2)}, u32[]{:S(2)}) %collective-permute-start.43) | collective-permute-done | bytes 262176 | tf_op jit(solution)/shard_map/ppermute | solution.py:35
  287.6 4.6 %collective-permute-start.48 = (f32[32,1024]{1,0:T(8,128)S(1)}, f32[32,1024]{1,0:T(8,128)S(1)}, u32[]{:S(2)}, u32[]{:S(2)}) collective-permute-start(f32[32,1024]{1,0:T(8,128)S(1)} %get-tuple-element.87), channel_id=1, source_target_pairs={{0,68},{1,69},{2,70},{3,71},{4,64},{5,65},{6,66},{7,67},{8,76},{9,... | collective-permute-start | bytes 393224 | tf_op jit(solution)/shard_map/ppermute | solution.py:35
  (230 shorter events, 120.7 us)
Async XLA Ops:
  36.9 46.6 %collective-permute-start.9 = (bf16[2,128,4096]{2,1,0:T(8,128)(2,1)}, bf16[2,128,4096]{2,1,0:T(8,128)(2,1)}, u32[]{:S(2)}, u32[]{:S(2)}) collective-permute-start(bf16[2,128,4096]{2,1,0:T(8,128)(2,1)} %shard_map.82.refs_0_), channel_id=1, source_target_pairs={{0,16},{1,17},{2,18},{3,19},{4,20},{5,21},{6,22},{7,23},{8,24},{9,... | collective-permute-start | bytes 6291464 | tf_op jit(solution)/shard_map/ppermute | solution.py:35
  38.9 18.1 %collective-permute-start.13 = (bf16[2,128,1024]{2,1,0:T(8,128)(2,1)S(1)}, bf16[2,128,1024]{2,1,0:T(8,128)(2,1)S(1)}, u32[]{:S(2)}, u32[]{:S(2)}) collective-permute-start(bf16[2,128,1024]{2,1,0:T(8,128)(2,1)S(1)} %shard_map.83.refs_7_.refs_13_), channel_id=1, source_target_pairs={{0,4},{1,5},{2,6},{3,7},{8,12},{9,13},{10,14},{11,15},{16,20},{17,... | collective-permute-start | bytes 1572872 | tf_op jit(solution)/shard_map/ppermute | solution.py:35
  44.0 16.2 %collective-permute-start.10 = (bf16[2,128,1024]{2,1,0:T(8,128)(2,1)S(1)}, bf16[2,128,1024]{2,1,0:T(8,128)(2,1)}, u32[]{:S(2)}, u32[]{:S(2)}) collective-permute-start(bf16[2,128,1024]{2,1,0:T(8,128)(2,1)S(1)} %shard_map.83.refs_7_.refs_13_), channel_id=1, source_target_pairs={{0,1},{1,2},{2,3},{4,5},{5,6},{6,7},{8,9},{9,10},{10,11},{12,13},{... | collective-permute-start | bytes 1572872 | tf_op jit(solution)/shard_map/ppermute | solution.py:35
  48.7 19.7 %collective-permute-start.11 = (bf16[2,128,1024]{2,1,0:T(8,128)(2,1)S(1)}, bf16[2,128,1024]{2,1,0:T(8,128)(2,1)S(1)}, u32[]{:S(2)}, u32[]{:S(2)}) collective-permute-start(bf16[2,128,1024]{2,1,0:T(8,128)(2,1)S(1)} %shard_map.83.refs_7_.refs_13_), channel_id=1, source_target_pairs={{0,2},{1,3},{4,6},{5,7},{8,10},{9,11},{12,14},{13,15},{16,18},{17,... | collective-permute-start | bytes 1572872 | tf_op jit(solution)/shard_map/ppermute | solution.py:35
  54.8 17.2 %collective-permute-start.12 = (bf16[2,128,1024]{2,1,0:T(8,128)(2,1)S(1)}, bf16[2,128,1024]{2,1,0:T(8,128)(2,1)S(1)}, u32[]{:S(2)}, u32[]{:S(2)}) collective-permute-start(bf16[2,128,1024]{2,1,0:T(8,128)(2,1)S(1)} %shard_map.83.refs_7_.refs_13_), channel_id=1, source_target_pairs={{0,3},{4,7},{8,11},{12,15},{16,19},{20,23},{24,27},{28,31},{32,35}... | collective-permute-start | bytes 1572872 | tf_op jit(solution)/shard_map/ppermute | solution.py:35
  88.5 35.8 %collective-permute-start.17 = (bf16[2,128,2048]{2,1,0:T(8,128)(2,1)}, bf16[2,128,2048]{2,1,0:T(8,128)(2,1)}, u32[]{:S(2)}, u32[]{:S(2)}) collective-permute-start(bf16[2,128,2048]{2,1,0:T(8,128)(2,1)} %get-tuple-element.48.refs_8_), channel_id=1, source_target_pairs={{0,32},{1,33},{2,34},{3,35},{4,36},{5,37},{6,38},{7,39},{8,40},{9,... | collective-permute-start | bytes 3145736 | tf_op jit(solution)/shard_map/ppermute | solution.py:35
  95.7 28.5 %collective-permute-start.18 = (bf16[2,256,512]{2,1,0:T(8,128)(2,1)S(1)}, bf16[2,256,512]{2,1,0:T(8,128)(2,1)S(1)}, u32[]{:S(2)}, u32[]{:S(2)}) collective-permute-start(bf16[2,256,512]{2,1,0:T(8,128)(2,1)S(1)} %get-tuple-element.52), channel_id=1, source_target_pairs={{0,32},{1,33},{2,34},{3,35},{4,36},{5,37},{6,38},{7,39},{8,40},{9,... | collective-permute-start | bytes 1572872 | tf_op jit(solution)/shard_map/ppermute | solution.py:35
  127.0 23.9 %collective-permute-start.19 = (bf16[2,128,2048]{2,1,0:T(8,128)(2,1)}, bf16[2,128,2048]{2,1,0:T(8,128)(2,1)}, u32[]{:S(2)}, u32[]{:S(2)}) collective-permute-start(bf16[2,128,2048]{2,1,0:T(8,128)(2,1)} %shard_map.88), channel_id=1, source_target_pairs={{0,32},{1,33},{2,34},{3,35},{4,36},{5,37},{6,38},{7,39},{8,40},{9,... | collective-permute-start | bytes 3145736 | tf_op jit(solution)/shard_map/ppermute | solution.py:35
  151.8 17.5 %collective-permute-start.23 = (bf16[256,512]{1,0:T(8,128)(2,1)S(1)}, bf16[256,512]{1,0:T(8,128)(2,1)S(1)}, u32[]{:S(2)}, u32[]{:S(2)}) collective-permute-start(bf16[256,512]{1,0:T(8,128)(2,1)S(1)} %get-tuple-element.95), channel_id=1, source_target_pairs={{0,8},{1,9},{2,10},{3,11},{4,12},{5,13},{6,14},{7,15},{8,0},{9,1},... | collective-permute-start | bytes 786440 | tf_op jit(solution)/shard_map/ppermute | solution.py:35
  151.9 16.6 %collective-permute-start.27 = (bf16[2,256,512]{2,1,0:T(8,128)(2,1)S(1)}, bf16[2,256,512]{2,1,0:T(8,128)(2,1)S(1)}, u32[]{:S(2)}, u32[]{:S(2)}) collective-permute-start(bf16[2,256,512]{2,1,0:T(8,128)(2,1)S(1)} %get-tuple-element.72), channel_id=1, source_target_pairs={{0,48},{1,49},{2,50},{3,51},{4,52},{5,53},{6,54},{7,55},{8,56},{9,... | collective-permute-start | bytes 1572872 | tf_op jit(solution)/shard_map/ppermute | solution.py:35
  166.5 16.1 %collective-permute-start.22 = (bf16[2,128,512]{2,1,0:T(8,128)(2,1)S(1)}, bf16[2,128,512]{2,1,0:T(8,128)(2,1)S(1)}, u32[]{:S(2)}, u32[]{:S(2)}) collective-permute-start(bf16[2,128,512]{2,1,0:T(8,128)(2,1)S(1)} %get-tuple-element.68), channel_id=1, source_target_pairs={{3,0},{4,1},{5,2},{6,3},{7,4},{11,8},{12,9},{13,10},{14,11},{15,12... | collective-permute-start | bytes 786440 | tf_op jit(solution)/shard_map/ppermute | solution.py:35
  168.5 21.9 %collective-permute-start.26 = (bf16[256,512]{1,0:T(8,128)(2,1)S(1)}, bf16[256,512]{1,0:T(8,128)(2,1)S(1)}, u32[]{:S(2)}, u32[]{:S(2)}) collective-permute-start(bf16[256,512]{1,0:T(8,128)(2,1)S(1)} %get-tuple-element.91), channel_id=1, source_target_pairs={{0,8},{1,9},{2,10},{3,11},{4,12},{5,13},{6,14},{7,15},{8,0},{9,1},... | collective-permute-start | bytes 786440 | tf_op jit(solution)/shard_map/ppermute | solution.py:35
  170.0 28.2 %collective-permute-start.29 = (bf16[2,128,512]{2,1,0:T(8,128)(2,1)S(1)}, bf16[2,128,512]{2,1,0:T(8,128)(2,1)S(1)}, u32[]{:S(2)}, u32[]{:S(2)}) collective-permute-start(bf16[2,128,512]{2,1,0:T(8,128)(2,1)S(1)} %get-tuple-element.74), channel_id=1, source_target_pairs={{4,0},{5,1},{6,2},{7,3},{12,8},{13,9},{14,10},{15,11},{20,16},{21,... | collective-permute-start | bytes 786440 | tf_op jit(solution)/shard_map/ppermute | solution.py:35
  174.2 28.6 %collective-permute-start.30 = (bf16[2,128,512]{2,1,0:T(8,128)(2,1)S(1)}, bf16[2,128,512]{2,1,0:T(8,128)(2,1)S(1)}, u32[]{:S(2)}, u32[]{:S(2)}) collective-permute-start(bf16[2,128,512]{2,1,0:T(8,128)(2,1)S(1)} %get-tuple-element.75), channel_id=1, source_target_pairs={{5,0},{6,1},{7,2},{13,8},{14,9},{15,10},{21,16},{22,17},{23,18},{2... | collective-permute-start | bytes 786440 | tf_op jit(solution)/shard_map/ppermute | solution.py:35
  177.1 27.7 %collective-permute-start.25 = (bf16[256,512]{1,0:T(8,128)(2,1)S(1)}, bf16[256,512]{1,0:T(8,128)(2,1)S(1)}, u32[]{:S(2)}, u32[]{:S(2)}) collective-permute-start(bf16[256,512]{1,0:T(8,128)(2,1)S(1)} %get-tuple-element.93), channel_id=1, source_target_pairs={{0,8},{1,9},{2,10},{3,11},{4,12},{5,13},{6,14},{7,15},{8,0},{9,1},... | collective-permute-start | bytes 786440 | tf_op jit(solution)/shard_map/ppermute | solution.py:35
  182.6 24.2 %collective-permute-start.28 = (bf16[256,512]{1,0:T(8,128)(2,1)S(1)}, bf16[256,512]{1,0:T(8,128)(2,1)S(1)}, u32[]{:S(2)}, u32[]{:S(2)}) collective-permute-start(bf16[256,512]{1,0:T(8,128)(2,1)S(1)} %get-tuple-element.89), channel_id=1, source_target_pairs={{0,8},{1,9},{2,10},{3,11},{4,12},{5,13},{6,14},{7,15},{8,0},{9,1},... | collective-permute-start | bytes 786440 | tf_op jit(solution)/shard_map/ppermute | solution.py:35
  191.1 26.2 %collective-permute-start.31 = (bf16[2,128,512]{2,1,0:T(8,128)(2,1)}, bf16[2,128,512]{2,1,0:T(8,128)(2,1)S(1)}, u32[]{:S(2)}, u32[]{:S(2)}) collective-permute-start(bf16[2,128,512]{2,1,0:T(8,128)(2,1)} %get-tuple-element.77), channel_id=1, source_target_pairs={{1,0},{2,1},{3,2},{4,3},{5,4},{6,5},{7,6},{9,8},{10,9},{11,10},{12... | collective-permute-start | bytes 786440 | tf_op jit(solution)/shard_map/ppermute | solution.py:35
  198.8 18.4 %collective-permute-start.32 = (bf16[2,128,512]{2,1,0:T(8,128)(2,1)}, bf16[2,128,512]{2,1,0:T(8,128)(2,1)S(1)}, u32[]{:S(2)}, u32[]{:S(2)}) collective-permute-start(bf16[2,128,512]{2,1,0:T(8,128)(2,1)} %get-tuple-element.78), channel_id=1, source_target_pairs={{2,0},{3,1},{4,2},{5,3},{6,4},{7,5},{10,8},{11,9},{12,10},{13,11},... | collective-permute-start | bytes 786440 | tf_op jit(solution)/shard_map/ppermute | solution.py:35
  203.5 18.8 %collective-permute-start.33 = (bf16[2,128,512]{2,1,0:T(8,128)(2,1)}, bf16[2,128,512]{2,1,0:T(8,128)(2,1)S(1)}, u32[]{:S(2)}, u32[]{:S(2)}) collective-permute-start(bf16[2,128,512]{2,1,0:T(8,128)(2,1)} %get-tuple-element.79), channel_id=1, source_target_pairs={{3,0},{4,1},{5,2},{6,3},{7,4},{11,8},{12,9},{13,10},{14,11},{15,12... | collective-permute-start | bytes 786440 | tf_op jit(solution)/shard_map/ppermute | solution.py:35
  205.4 26.1 %collective-permute-start.34 = (bf16[2,128,512]{2,1,0:T(8,128)(2,1)}, bf16[2,128,512]{2,1,0:T(8,128)(2,1)S(1)}, u32[]{:S(2)}, u32[]{:S(2)}) collective-permute-start(bf16[2,128,512]{2,1,0:T(8,128)(2,1)} %get-tuple-element.80), channel_id=1, source_target_pairs={{4,0},{5,1},{6,2},{7,3},{12,8},{13,9},{14,10},{15,11},{20,16},{21,... | collective-permute-start | bytes 786440 | tf_op jit(solution)/shard_map/ppermute | solution.py:35
  207.4 29.3 %collective-permute-start.35 = (bf16[2,128,512]{2,1,0:T(8,128)(2,1)S(1)}, bf16[2,128,512]{2,1,0:T(8,128)(2,1)}, u32[]{:S(2)}, u32[]{:S(2)}) collective-permute-start(bf16[2,128,512]{2,1,0:T(8,128)(2,1)S(1)} %get-tuple-element.81), channel_id=1, source_target_pairs={{5,0},{6,1},{7,2},{13,8},{14,9},{15,10},{21,16},{22,17},{23,18},{2... | collective-permute-start | bytes 786440 | tf_op jit(solution)/shard_map/ppermute | solution.py:35
  239.6 23.5 %collective-permute-start.39 = (bf16[2,128,1024]{2,1,0:T(8,128)(2,1)S(1)}, bf16[2,128,1024]{2,1,0:T(8,128)(2,1)S(1)}, u32[]{:S(2)}, u32[]{:S(2)}) collective-permute-start(bf16[2,128,1024]{2,1,0:T(8,128)(2,1)S(1)} %shard_map.93.refs_0_), channel_id=1, source_target_pairs={{0,32},{1,33},{2,34},{3,35},{4,36},{5,37},{6,38},{7,39},{8,40},{9,... | collective-permute-start | bytes 1572872 | tf_op jit(solution)/shard_map/ppermute | solution.py:35
  240.4 25.3 %collective-permute-start.41 = (bf16[2,128,1024]{2,1,0:T(8,128)(2,1)S(1)}, bf16[2,128,1024]{2,1,0:T(8,128)(2,1)S(1)}, u32[]{:S(2)}, u32[]{:S(2)}) collective-permute-start(bf16[2,128,1024]{2,1,0:T(8,128)(2,1)S(1)} %shard_map.93.refs_0_), channel_id=1, source_target_pairs={{0,48},{1,49},{2,50},{3,51},{4,52},{5,53},{6,54},{7,55},{8,56},{9,... | collective-permute-start | bytes 1572872 | tf_op jit(solution)/shard_map/ppermute | solution.py:35
  242.9 22.8 %collective-permute-start.36 = (bf16[2,128,1024]{2,1,0:T(8,128)(2,1)S(1)}, bf16[2,128,1024]{2,1,0:T(8,128)(2,1)S(1)}, u32[]{:S(2)}, u32[]{:S(2)}) collective-permute-start(bf16[2,128,1024]{2,1,0:T(8,128)(2,1)S(1)} %shard_map.93.refs_0_), channel_id=1, source_target_pairs={{0,8},{1,9},{2,10},{3,11},{4,12},{5,13},{6,14},{7,15},{8,0},{9,1},... | collective-permute-start | bytes 1572872 | tf_op jit(solution)/shard_map/ppermute | solution.py:35
  (81 other events, 696.7 us)

commit v2 on v0

--- a/solution.py
+++ b/solution.py
@@ -440,19 +440,10 @@
 
 def product_kernel(x_ref, *refs):
     grads, outs = refs[:TEAM], refs[TEAM:]
+    rows = jnp.concatenate([grad[slot] for grad in grads for slot in range(2)], axis=0)
+    total = jnp.dot(x_ref[...], rows, preferred_element_type=jnp.float32)
     for z, out in enumerate(outs):
-        rows = slice(z * 4 * 32, (z + 1) * 4 * 32)
-        total = None
-        for rel, grad in enumerate(grads):
-            span = 2 * BLOCK
-            block = jnp.concatenate([grad[0], grad[1]], axis=0)
-            term = jnp.dot(
-                x_ref[rows, rel * span : (rel + 1) * span],
-                block,
-                preferred_element_type=jnp.float32,
-            )
-            total = term if total is None else total + term
-        out[...] = total.astype(out.dtype)
+        out[...] = total[z * 4 * 32 : (z + 1) * 4 * 32].astype(out.dtype)
 
 
 def product(x, grads):

time: 267 us -> 268 us (level)
  transfers between devices with their start and end apart: 49 -> 49, of which waited for: 31 -> 32; matrix products, arithmetic and copies ran while one was open for 4% -> 4% of each run, Pallas kernels for 13% -> 14%
where the time goes in v2:
time: 268 us; the launch traced here: 266 us
  waiting for transfers between devices  119 us (44%)
  starting transfers between devices  68.2 us (25%)
  Pallas kernels  51 us (19%)
  local copies, waits for them, and re-layouts  11.8 us (4%)
  matrix products  6.49 us (2%)
  between operations  5.12 us (2%)
  other arithmetic  4.84 us (2%)
    ppermute x49, waiting for transfers between devices, move(): return lax.ppermute(value, AXES, route)  119 us
    ppermute x49, starting transfers between devices, move(): return lax.ppermute(value, AXES, route)  68.2 us
    pallas_call x4, Pallas kernels, attention(): pl.pallas_call(attention_kernel, grid_spec=spec, out_shape=[jax.ShapeDtyp...  30.5 us
    pallas_call x8, Pallas kernels, copier(): pl.pallas_call(kernel, in_specs=[pl.BlockSpec(memory_space=pltpu.SMEM)] +...  13.6 us
    unnamed x84, local copies, waits for them, and re-layouts  10.3 us
    dot_general x1, matrix products, per_device(): jnp.dot(flat, kv_weight, preferred_element_type=jnp.float32)  6.49 us
  transfers between devices with their start and end apart: 49, of which 32 were waited for; matrix products, arithmetic and copies ran while one was open for 4% of the time, Pallas kernels for 14%

profile of v2, /device:TPU:0, one launch (start us, length us, event | category | flops | bytes accessed | tf_op | source)
XLA Modules:
  0.0 266.2 jit_solution(6086640905706417618)
XLA Ops:
  5.0 6.5 %convolution_convert_fusion = bf16[256,1024]{1,0:T(8,128)(2,1)S(1)} fusion(bf16[256,4096]{1,0:T(8,128)(2,1)} %bitcast.41, bf16[4096,1024]{1,0:T(8,128)(2,1)} %param.9), kind=kOutput, calls=%fused_computation | convolution fusion | flops 2147745792 | bytes 11010048 | tf_op jit(solution)/shard_map/dot_general | solution.py:498
  20.1 6.6 %collective-permute-done.7.came_ref = bf16[1,128,1024]{2,1,0:T(8,128)(2,1)S(1)} collective-permute-done((bf16[1,128,1024]{2,1,0:T(8,128)(2,1)S(1)}, bf16[1,128,1024]{2,1,0:T(8,128)(2,1)S(1)}, u32[]{:S(2)}, u32[]{:S(2)}) %collective-permute-start.7) | collective-permute-done | bytes 262176 | tf_op jit(solution)/shard_map/ppermute | solution.py:35
  30.8 3.6 %shard_map.80.refs_0_ = bf16[2,128,4096]{2,1,0:T(8,128)(2,1)} custom-call(s32[3]{0:T(128)S(1)} %bitcast.69, bf16[128,4096]{1,0:T(8,128)(2,1)S(1)} %collective-permute-done.5.refs_0_, bf16[128,4096]{1,0:T(8,128)(2,1)S(1)} %collective-permute-done.6.refs_1_, bf16[2,128,4096]{2,1,0:T(8,128)(2,1)} %refs_2_.5, bf16[2,128,4096]{2,1,0:T(8,128)(2,1)} %refs_3_.5), custom_call_target="tpu_custom_call" | custom-call | bytes 4194304 | tf_op jit(solution)/shard_map/pallas_call | solution.py:92
  38.9 5.1 %collective-permute-start.13 = (bf16[2,128,1024]{2,1,0:T(8,128)(2,1)S(1)}, bf16[2,128,1024]{2,1,0:T(8,128)(2,1)S(1)}, u32[]{:S(2)}, u32[]{:S(2)}) collective-permute-start(bf16[2,128,1024]{2,1,0:T(8,128)(2,1)S(1)} %shard_map.83.refs_7_.refs_13_), channel_id=1, source_target_pairs={{0,4},{1,5},{2,6},{3,7},{8,12},{9,13},{10,14},{11,15},{16,20},{17,... | collective-permute-start | bytes 1572872 | tf_op jit(solution)/shard_map/ppermute | solution.py:35
  44.0 4.6 %collective-permute-start.10 = (bf16[2,128,1024]{2,1,0:T(8,128)(2,1)S(1)}, bf16[2,128,1024]{2,1,0:T(8,128)(2,1)}, u32[]{:S(2)}, u32[]{:S(2)}) collective-permute-start(bf16[2,128,1024]{2,1,0:T(8,128)(2,1)S(1)} %shard_map.83.refs_7_.refs_13_), channel_id=1, source_target_pairs={{0,1},{1,2},{2,3},{4,5},{5,6},{6,7},{8,9},{9,10},{10,11},{12,13},{... | collective-permute-start | bytes 1572872 | tf_op jit(solution)/shard_map/ppermute | solution.py:35
  48.7 4.7 %collective-permute-start.11 = (bf16[2,128,1024]{2,1,0:T(8,128)(2,1)S(1)}, bf16[2,128,1024]{2,1,0:T(8,128)(2,1)S(1)}, u32[]{:S(2)}, u32[]{:S(2)}) collective-permute-start(bf16[2,128,1024]{2,1,0:T(8,128)(2,1)S(1)} %shard_map.83.refs_7_.refs_13_), channel_id=1, source_target_pairs={{0,2},{1,3},{4,6},{5,7},{8,10},{9,11},{12,14},{13,15},{16,18},{17,... | collective-permute-start | bytes 1572872 | tf_op jit(solution)/shard_map/ppermute | solution.py:35
  60.9 7.4 %collective-permute-done.11.refs_5_ = bf16[2,128,1024]{2,1,0:T(8,128)(2,1)S(1)} collective-permute-done((bf16[2,128,1024]{2,1,0:T(8,128)(2,1)S(1)}, bf16[2,128,1024]{2,1,0:T(8,128)(2,1)S(1)}, u32[]{:S(2)}, u32[]{:S(2)}) %collective-permute-start.11) | collective-permute-done | bytes 524320 | tf_op jit(solution)/shard_map/ppermute | solution.py:35
  72.1 11.4 %collective-permute-done.9.came_ref = bf16[2,128,4096]{2,1,0:T(8,128)(2,1)} collective-permute-done((bf16[2,128,4096]{2,1,0:T(8,128)(2,1)}, bf16[2,128,4096]{2,1,0:T(8,128)(2,1)}, u32[]{:S(2)}, u32[]{:S(2)}) %collective-permute-start.9) | collective-permute-done | bytes 2097184 | tf_op jit(solution)/shard_map/ppermute | solution.py:35
  83.5 4.1 %shard_map.84 = (bf16[2,128,2048]{2,1,0:T(8,128)(2,1)}, bf16[2,128,4096]{2,1,0:T(8,128)(2,1)}) custom-call(s32[3]{0:T(128)S(1)} %bitcast.71, bf16[2,128,4096]{2,1,0:T(8,128)(2,1)} %collective-permute-done.9.came_ref, bf16[128,4096]{1,0:T(8,128)(2,1)S(1)} %collective-permute-done.5.refs_0_, bf16[128,4096]{1,0:T(8,128)(2,1)} %copy-done.15, ...), custom_call_target="tpu_custom_call" | custom-call | bytes 4194304 | tf_op jit(solution)/shard_map/pallas_call | solution.py:92
  97.3 7.6 %shard_map.85 = (bf16[2,128,4096]{2,1,0:T(8,128)(2,1)}, bf16[2,128,512]{2,1,0:T(8,128)(2,1)}, bf16[2,128,512]{2,1,0:T(8,128)(2,1)}, bf16[2,128,512]{2,1,0:T(8,12...) custom-call(s32[2]{0:T(128)S(1)} %pad_add_fusion.3.info_ref, ...), custom_call_target="tpu_custom_call" | custom-call | flops 2013265920 | bytes 4194304 | tf_op jit(solution)/shard_map/pallas_call | solution.py:388
  105.6 7.6 %shard_map.86 = (bf16[2,128,4096]{2,1,0:T(8,128)(2,1)}, bf16[2,128,512]{2,1,0:T(8,128)(2,1)S(1)}, bf16[2,128,512]{2,1,0:T(8,128)(2,1)S(1)}, bf16[2,128,512]{2,1,...) custom-call(s32[2]{0:T(128)S(1)} %pad_add_fusion.3.info_ref, ...), custom_call_target="tpu_custom_call", output_to_operand_aliasing={{0}: (16, {})} | custom-call | flops 2013265920 | bytes 4194304 | tf_op jit(solution)/shard_map/pallas_call | solution.py:388
  114.0 10.2 %collective-permute-done.18.refs_6_ = bf16[2,256,512]{2,1,0:T(8,128)(2,1)S(1)} collective-permute-done((bf16[2,256,512]{2,1,0:T(8,128)(2,1)S(1)}, bf16[2,256,512]{2,1,0:T(8,128)(2,1)S(1)}, u32[]{:S(2)}, u32[]{:S(2)}) %collective-permute-start.18) | collective-permute-done | bytes 524320 | tf_op jit(solution)/shard_map/ppermute | solution.py:35
  137.0 7.6 %shard_map.89 = (bf16[2,128,4096]{2,1,0:T(8,128)(2,1)}, bf16[2,128,512]{2,1,0:T(8,128)(2,1)}, bf16[2,128,512]{2,1,0:T(8,128)(2,1)}, bf16[2,128,512]{2,1,0:T(8,12...) custom-call(s32[2]{0:T(128)S(1)} %pad_add_fusion.2.info_ref, ...), custom_call_target="tpu_custom_call", output_to_operand_aliasing={{0}: (16, {}), {1}: (17, {}), {2}: (18, {}), {3}: (19, {}),... | custom-call | flops 2013265920 | bytes 4194304 | tf_op jit(solution)/shard_map/pallas_call | solution.py:388
  153.3 6.9 %collective-permute-done.21.refs_23_.refs_2_ = bf16[2,128,512]{2,1,0:T(8,128)(2,1)S(1)} collective-permute-done((bf16[2,128,512]{2,1,0:T(8,128)(2,1)}, bf16[2,128,512]{2,1,0:T(8,128)(2,1)S(1)}, u32[]{:S(2)}, u32[]{:S(2)}) %collective-permute-start.21) | collective-permute-done | bytes 262176 | tf_op jit(solution)/shard_map/ppermute | solution.py:35
  161.3 7.7 %shard_map.91 = (bf16[2,128,4096]{2,1,0:T(8,128)(2,1)}, bf16[2,128,512]{2,1,0:T(8,128)(2,1)S(1)}, bf16[2,128,512]{2,1,0:T(8,128)(2,1)S(1)}, bf16[2,128,512]{2,1,...) custom-call(s32[2]{0:T(128)S(1)} %pad_add_fusion.2.info_ref, ...), custom_call_target="tpu_custom_call", output_to_operand_aliasing={{0}: (16, {}), {1}: (17, {}), {2}: (18, {}), {3}: (19, {}),... | custom-call | flops 2013265920 | bytes 4194304 | tf_op jit(solution)/shard_map/pallas_call | solution.py:388
  177.0 9.1 %collective-permute-done.31.refs_7_ = bf16[2,128,512]{2,1,0:T(8,128)(2,1)S(1)} collective-permute-done((bf16[2,128,512]{2,1,0:T(8,128)(2,1)S(1)}, bf16[2,128,512]{2,1,0:T(8,128)(2,1)S(1)}, u32[]{:S(2)}, u32[]{:S(2)}) %collective-permute-start.31) | collective-permute-done | bytes 262176 | tf_op jit(solution)/shard_map/ppermute | solution.py:35
  187.4 5.6 %collective-permute-done.32.refs_8_ = bf16[2,128,512]{2,1,0:T(8,128)(2,1)S(1)} collective-permute-done((bf16[2,128,512]{2,1,0:T(8,128)(2,1)S(1)}, bf16[2,128,512]{2,1,0:T(8,128)(2,1)S(1)}, u32[]{:S(2)}, u32[]{:S(2)}) %collective-permute-start.32) | collective-permute-done | bytes 262176 | tf_op jit(solution)/shard_map/ppermute | solution.py:35
  195.7 5.9 %collective-permute-done.34.refs_10_ = bf16[2,128,512]{2,1,0:T(8,128)(2,1)S(1)} collective-permute-done((bf16[2,128,512]{2,1,0:T(8,128)(2,1)S(1)}, bf16[2,128,512]{2,1,0:T(8,128)(2,1)S(1)}, u32[]{:S(2)}, u32[]{:S(2)}) %collective-permute-start.34) | collective-permute-done | bytes 262176 | tf_op jit(solution)/shard_map/ppermute | solution.py:35
  201.7 4.0 %collective-permute-done.35.refs_11_ = bf16[2,128,512]{2,1,0:T(8,128)(2,1)S(1)} collective-permute-done((bf16[2,128,512]{2,1,0:T(8,128)(2,1)S(1)}, bf16[2,128,512]{2,1,0:T(8,128)(2,1)S(1)}, u32[]{:S(2)}, u32[]{:S(2)}) %collective-permute-start.35) | collective-permute-done | bytes 262176 | tf_op jit(solution)/shard_map/ppermute | solution.py:35
  213.2 6.9 %collective-permute-done.37.refs_2_ = bf16[2,128,1024]{2,1,0:T(8,128)(2,1)S(1)} collective-permute-done((bf16[2,128,1024]{2,1,0:T(8,128)(2,1)S(1)}, bf16[2,128,1024]{2,1,0:T(8,128)(2,1)S(1)}, u32[]{:S(2)}, u32[]{:S(2)}) %collective-permute-start.37) | collective-permute-done | bytes 524320 | tf_op jit(solution)/shard_map/ppermute | solution.py:35
  220.1 6.1 %collective-permute-done.39.refs_4_ = bf16[2,128,1024]{2,1,0:T(8,128)(2,1)} collective-permute-done((bf16[2,128,1024]{2,1,0:T(8,128)(2,1)S(1)}, bf16[2,128,1024]{2,1,0:T(8,128)(2,1)}, u32[]{:S(2)}, u32[]{:S(2)}) %collective-permute-start.39) | collective-permute-done | bytes 524320 | tf_op jit(solution)/shard_map/ppermute | solution.py:35
  233.8 4.8 %shard_map.94 = (f32[128,1024]{1,0:T(8,128)S(1)}, bf16[128,1024]{1,0:T(8,128)(2,1)S(1)}, bf16[128,1024]{1,0:T(8,128)(2,1)S(1)}, bf16[128,1024]{1,0:T(8,128)(2,1)S(1)}) custom-call(bf16[512,2048]{1,0:T(8,128)(2,1)} %copy-done.21, bf16[2,128,1024]{2,1,0:T(8,128)(2,1)S(1)} %shard_map.93.refs_0_, bf16[2,128,1024]{2,1,0:T(8,128)(2,1)} %collective-permute-done.36.refs_1_, ...), custom_call_target="tpu_custom_call" | custom-call | flops 2147483648 | bytes 5242880 | tf_op jit(solution)/shard_map/pallas_call | solution.py:452
  243.4 4.5 %collective-permute-done.43 = bf16[128,1024]{1,0:T(8,128)(2,1)S(1)} collective-permute-done((bf16[128,1024]{1,0:T(8,128)(2,1)S(1)}, bf16[128,1024]{1,0:T(8,128)(2,1)S(1)}, u32[]{:S(2)}, u32[]{:S(2)}) %collective-permute-start.43) | collective-permute-done | bytes 262176 | tf_op jit(solution)/shard_map/ppermute | solution.py:35
  247.8 5.2 %collective-permute-done.44 = bf16[128,1024]{1,0:T(8,128)(2,1)S(1)} collective-permute-done((bf16[128,1024]{1,0:T(8,128)(2,1)S(1)}, bf16[128,1024]{1,0:T(8,128)(2,1)S(1)}, u32[]{:S(2)}, u32[]{:S(2)}) %collective-permute-start.44) | collective-permute-done | bytes 262176 | tf_op jit(solution)/shard_map/ppermute | solution.py:35
  (202 shorter events, 107.2 us)
Async XLA Ops:
  36.9 46.6 %collective-permute-start.9 = (bf16[2,128,4096]{2,1,0:T(8,128)(2,1)}, bf16[2,128,4096]{2,1,0:T(8,128)(2,1)}, u32[]{:S(2)}, u32[]{:S(2)}) collective-permute-start(bf16[2,128,4096]{2,1,0:T(8,128)(2,1)} %shard_map.82.refs_0_), channel_id=1, source_target_pairs={{0,16},{1,17},{2,18},{3,19},{4,20},{5,21},{6,22},{7,23},{8,24},{9,... | collective-permute-start | bytes 6291464 | tf_op jit(solution)/shard_map/ppermute | solution.py:35
  38.9 18.0 %collective-permute-start.13 = (bf16[2,128,1024]{2,1,0:T(8,128)(2,1)S(1)}, bf16[2,128,1024]{2,1,0:T(8,128)(2,1)S(1)}, u32[]{:S(2)}, u32[]{:S(2)}) collective-permute-start(bf16[2,128,1024]{2,1,0:T(8,128)(2,1)S(1)} %shard_map.83.refs_7_.refs_13_), channel_id=1, source_target_pairs={{0,4},{1,5},{2,6},{3,7},{8,12},{9,13},{10,14},{11,15},{16,20},{17,... | collective-permute-start | bytes 1572872 | tf_op jit(solution)/shard_map/ppermute | solution.py:35
  44.0 16.2 %collective-permute-start.10 = (bf16[2,128,1024]{2,1,0:T(8,128)(2,1)S(1)}, bf16[2,128,1024]{2,1,0:T(8,128)(2,1)}, u32[]{:S(2)}, u32[]{:S(2)}) collective-permute-start(bf16[2,128,1024]{2,1,0:T(8,128)(2,1)S(1)} %shard_map.83.refs_7_.refs_13_), channel_id=1, source_target_pairs={{0,1},{1,2},{2,3},{4,5},{5,6},{6,7},{8,9},{9,10},{10,11},{12,13},{... | collective-permute-start | bytes 1572872 | tf_op jit(solution)/shard_map/ppermute | solution.py:35
  48.7 19.7 %collective-permute-start.11 = (bf16[2,128,1024]{2,1,0:T(8,128)(2,1)S(1)}, bf16[2,128,1024]{2,1,0:T(8,128)(2,1)S(1)}, u32[]{:S(2)}, u32[]{:S(2)}) collective-permute-start(bf16[2,128,1024]{2,1,0:T(8,128)(2,1)S(1)} %shard_map.83.refs_7_.refs_13_), channel_id=1, source_target_pairs={{0,2},{1,3},{4,6},{5,7},{8,10},{9,11},{12,14},{13,15},{16,18},{17,... | collective-permute-start | bytes 1572872 | tf_op jit(solution)/shard_map/ppermute | solution.py:35
  54.8 17.2 %collective-permute-start.12 = (bf16[2,128,1024]{2,1,0:T(8,128)(2,1)S(1)}, bf16[2,128,1024]{2,1,0:T(8,128)(2,1)S(1)}, u32[]{:S(2)}, u32[]{:S(2)}) collective-permute-start(bf16[2,128,1024]{2,1,0:T(8,128)(2,1)S(1)} %shard_map.83.refs_7_.refs_13_), channel_id=1, source_target_pairs={{0,3},{4,7},{8,11},{12,15},{16,19},{20,23},{24,27},{28,31},{32,35}... | collective-permute-start | bytes 1572872 | tf_op jit(solution)/shard_map/ppermute | solution.py:35
  56.9 15.1 %collective-permute-start.14 = (bf16[2,128,1024]{2,1,0:T(8,128)(2,1)S(1)}, bf16[2,128,1024]{2,1,0:T(8,128)(2,1)S(1)}, u32[]{:S(2)}, u32[]{:S(2)}) collective-permute-start(bf16[2,128,1024]{2,1,0:T(8,128)(2,1)S(1)} %collective-permute-done.13.refs_3_.refs_9_), channel_id=1, source_target_pairs={{4,5},{5,6},{6,7},{7,4},{12,13},{13,14},{14,15},{15,12},{20,21},{2... | collective-permute-start | bytes 1572872 | tf_op jit(solution)/shard_map/ppermute | solution.py:35
  88.5 35.7 %collective-permute-start.17 = (bf16[2,128,2048]{2,1,0:T(8,128)(2,1)}, bf16[2,128,2048]{2,1,0:T(8,128)(2,1)}, u32[]{:S(2)}, u32[]{:S(2)}) collective-permute-start(bf16[2,128,2048]{2,1,0:T(8,128)(2,1)} %get-tuple-element.48.refs_8_), channel_id=1, source_target_pairs={{0,32},{1,33},{2,34},{3,35},{4,36},{5,37},{6,38},{7,39},{8,40},{9,... | collective-permute-start | bytes 3145736 | tf_op jit(solution)/shard_map/ppermute | solution.py:35
  95.8 28.3 %collective-permute-start.18 = (bf16[2,256,512]{2,1,0:T(8,128)(2,1)S(1)}, bf16[2,256,512]{2,1,0:T(8,128)(2,1)S(1)}, u32[]{:S(2)}, u32[]{:S(2)}) collective-permute-start(bf16[2,256,512]{2,1,0:T(8,128)(2,1)S(1)} %get-tuple-element.52), channel_id=1, source_target_pairs={{0,32},{1,33},{2,34},{3,35},{4,36},{5,37},{6,38},{7,39},{8,40},{9,... | collective-permute-start | bytes 1572872 | tf_op jit(solution)/shard_map/ppermute | solution.py:35
  125.9 24.8 %collective-permute-start.19 = (bf16[2,128,2048]{2,1,0:T(8,128)(2,1)}, bf16[2,128,2048]{2,1,0:T(8,128)(2,1)}, u32[]{:S(2)}, u32[]{:S(2)}) collective-permute-start(bf16[2,128,2048]{2,1,0:T(8,128)(2,1)} %shard_map.88), channel_id=1, source_target_pairs={{0,32},{1,33},{2,34},{3,35},{4,36},{5,37},{6,38},{7,39},{8,40},{9,... | collective-permute-start | bytes 3145736 | tf_op jit(solution)/shard_map/ppermute | solution.py:35
  145.9 14.3 %collective-permute-start.21 = (bf16[2,128,512]{2,1,0:T(8,128)(2,1)}, bf16[2,128,512]{2,1,0:T(8,128)(2,1)S(1)}, u32[]{:S(2)}, u32[]{:S(2)}) collective-permute-start(bf16[2,128,512]{2,1,0:T(8,128)(2,1)} %get-tuple-element.67), channel_id=1, source_target_pairs={{2,0},{3,1},{4,2},{5,3},{6,4},{7,5},{10,8},{11,9},{12,10},{13,11},... | collective-permute-start | bytes 786440 | tf_op jit(solution)/shard_map/ppermute | solution.py:35
  148.5 25.0 %collective-permute-start.29 = (bf16[2,128,512]{2,1,0:T(8,128)(2,1)}, bf16[2,128,512]{2,1,0:T(8,128)(2,1)S(1)}, u32[]{:S(2)}, u32[]{:S(2)}) collective-permute-start(bf16[2,128,512]{2,1,0:T(8,128)(2,1)} %get-tuple-element.74), channel_id=1, source_target_pairs={{4,0},{5,1},{6,2},{7,3},{12,8},{13,9},{14,10},{15,11},{20,16},{21,... | collective-permute-start | bytes 786440 | tf_op jit(solution)/shard_map/ppermute | solution.py:35
  150.7 25.0 %collective-permute-start.30 = (bf16[2,128,512]{2,1,0:T(8,128)(2,1)}, bf16[2,128,512]{2,1,0:T(8,128)(2,1)S(1)}, u32[]{:S(2)}, u32[]{:S(2)}) collective-permute-start(bf16[2,128,512]{2,1,0:T(8,128)(2,1)} %get-tuple-element.75), channel_id=1, source_target_pairs={{5,0},{6,1},{7,2},{13,8},{14,9},{15,10},{21,16},{22,17},{23,18},{2... | collective-permute-start | bytes 786440 | tf_op jit(solution)/shard_map/ppermute | solution.py:35
  168.9 17.2 %collective-permute-start.31 = (bf16[2,128,512]{2,1,0:T(8,128)(2,1)S(1)}, bf16[2,128,512]{2,1,0:T(8,128)(2,1)S(1)}, u32[]{:S(2)}, u32[]{:S(2)}) collective-permute-start(bf16[2,128,512]{2,1,0:T(8,128)(2,1)S(1)} %get-tuple-element.77), channel_id=1, source_target_pairs={{1,0},{2,1},{3,2},{4,3},{5,4},{6,5},{7,6},{9,8},{10,9},{11,10},{12... | collective-permute-start | bytes 786440 | tf_op jit(solution)/shard_map/ppermute | solution.py:35
  170.2 22.8 %collective-permute-start.32 = (bf16[2,128,512]{2,1,0:T(8,128)(2,1)S(1)}, bf16[2,128,512]{2,1,0:T(8,128)(2,1)S(1)}, u32[]{:S(2)}, u32[]{:S(2)}) collective-permute-start(bf16[2,128,512]{2,1,0:T(8,128)(2,1)S(1)} %get-tuple-element.78), channel_id=1, source_target_pairs={{2,0},{3,1},{4,2},{5,3},{6,4},{7,5},{10,8},{11,9},{12,10},{13,11},... | collective-permute-start | bytes 786440 | tf_op jit(solution)/shard_map/ppermute | solution.py:35
  171.5 34.2 %collective-permute-start.24 = (bf16[2,256,512]{2,1,0:T(8,128)(2,1)S(1)}, bf16[2,256,512]{2,1,0:T(8,128)(2,1)S(1)}, u32[]{:S(2)}, u32[]{:S(2)}) collective-permute-start(bf16[2,256,512]{2,1,0:T(8,128)(2,1)S(1)} %get-tuple-element.69.refs_25_), channel_id=1, source_target_pairs={{0,16},{1,17},{2,18},{3,19},{4,20},{5,21},{6,22},{7,23},{8,24},{9,... | collective-permute-start | bytes 1572872 | tf_op jit(solution)/shard_map/ppermute | solution.py:35
  173.5 32.2 %collective-permute-start.27 = (bf16[2,256,512]{2,1,0:T(8,128)(2,1)S(1)}, bf16[2,256,512]{2,1,0:T(8,128)(2,1)S(1)}, u32[]{:S(2)}, u32[]{:S(2)}) collective-permute-start(bf16[2,256,512]{2,1,0:T(8,128)(2,1)S(1)} %get-tuple-element.72), channel_id=1, source_target_pairs={{0,48},{1,49},{2,50},{3,51},{4,52},{5,53},{6,54},{7,55},{8,56},{9,... | collective-permute-start | bytes 1572872 | tf_op jit(solution)/shard_map/ppermute | solution.py:35
  175.7 20.0 %collective-permute-start.33 = (bf16[2,128,512]{2,1,0:T(8,128)(2,1)S(1)}, bf16[2,128,512]{2,1,0:T(8,128)(2,1)S(1)}, u32[]{:S(2)}, u32[]{:S(2)}) collective-permute-start(bf16[2,128,512]{2,1,0:T(8,128)(2,1)S(1)} %get-tuple-element.79), channel_id=1, source_target_pairs={{3,0},{4,1},{5,2},{6,3},{7,4},{11,8},{12,9},{13,10},{14,11},{15,12... | collective-permute-start | bytes 786440 | tf_op jit(solution)/shard_map/ppermute | solution.py:35
  186.1 15.5 %collective-permute-start.34 = (bf16[2,128,512]{2,1,0:T(8,128)(2,1)S(1)}, bf16[2,128,512]{2,1,0:T(8,128)(2,1)S(1)}, u32[]{:S(2)}, u32[]{:S(2)}) collective-permute-start(bf16[2,128,512]{2,1,0:T(8,128)(2,1)S(1)} %get-tuple-element.80), channel_id=1, source_target_pairs={{4,0},{5,1},{6,2},{7,3},{12,8},{13,9},{14,10},{15,11},{20,16},{21,... | collective-permute-start | bytes 786440 | tf_op jit(solution)/shard_map/ppermute | solution.py:35
  206.2 19.9 %collective-permute-start.39 = (bf16[2,128,1024]{2,1,0:T(8,128)(2,1)S(1)}, bf16[2,128,1024]{2,1,0:T(8,128)(2,1)}, u32[]{:S(2)}, u32[]{:S(2)}) collective-permute-start(bf16[2,128,1024]{2,1,0:T(8,128)(2,1)S(1)} %shard_map.93.refs_0_), channel_id=1, source_target_pairs={{0,32},{1,33},{2,34},{3,35},{4,36},{5,37},{6,38},{7,39},{8,40},{9,... | collective-permute-start | bytes 1572872 | tf_op jit(solution)/shard_map/ppermute | solution.py:35
  208.6 20.1 %collective-permute-start.41 = (bf16[2,128,1024]{2,1,0:T(8,128)(2,1)S(1)}, bf16[2,128,1024]{2,1,0:T(8,128)(2,1)}, u32[]{:S(2)}, u32[]{:S(2)}) collective-permute-start(bf16[2,128,1024]{2,1,0:T(8,128)(2,1)S(1)} %shard_map.93.refs_0_), channel_id=1, source_target_pairs={{0,48},{1,49},{2,50},{3,51},{4,52},{5,53},{6,54},{7,55},{8,56},{9,... | collective-permute-start | bytes 1572872 | tf_op jit(solution)/shard_map/ppermute | solution.py:35
  212.6 16.2 %collective-permute-start.25 = (bf16[256,512]{1,0:T(8,128)(2,1)S(1)}, bf16[256,512]{1,0:T(8,128)(2,1)S(1)}, u32[]{:S(2)}, u32[]{:S(2)}) collective-permute-start(bf16[256,512]{1,0:T(8,128)(2,1)S(1)} %get-tuple-element.93), channel_id=1, source_target_pairs={{0,8},{1,9},{2,10},{3,11},{4,12},{5,13},{6,14},{7,15},{8,0},{9,1},... | collective-permute-start | bytes 786440 | tf_op jit(solution)/shard_map/ppermute | solution.py:35
  213.0 20.8 %collective-permute-start.36 = (bf16[2,128,1024]{2,1,0:T(8,128)(2,1)S(1)}, bf16[2,128,1024]{2,1,0:T(8,128)(2,1)}, u32[]{:S(2)}, u32[]{:S(2)}) collective-permute-start(bf16[2,128,1024]{2,1,0:T(8,128)(2,1)S(1)} %shard_map.93.refs_0_), channel_id=1, source_target_pairs={{0,8},{1,9},{2,10},{3,11},{4,12},{5,13},{6,14},{7,15},{8,0},{9,1},... | collective-permute-start | bytes 1572872 | tf_op jit(solution)/shard_map/ppermute | solution.py:35
  238.7 14.4 %collective-permute-start.44 = (bf16[128,1024]{1,0:T(8,128)(2,1)S(1)}, bf16[128,1024]{1,0:T(8,128)(2,1)S(1)}, u32[]{:S(2)}, u32[]{:S(2)}) collective-permute-start(bf16[128,1024]{1,0:T(8,128)(2,1)S(1)} %get-tuple-element.84), channel_id=1, source_target_pairs={{0,2},{1,3},{2,0},{3,1},{4,6},{5,7},{6,4},{7,5},{8,10},{9,11},{10,... | collective-permute-start | bytes 786440 | tf_op jit(solution)/shard_map/ppermute | solution.py:35
  240.8 14.9 %collective-permute-start.45 = (bf16[128,1024]{1,0:T(8,128)(2,1)S(1)}, bf16[128,1024]{1,0:T(8,128)(2,1)S(1)}, u32[]{:S(2)}, u32[]{:S(2)}) collective-permute-start(bf16[128,1024]{1,0:T(8,128)(2,1)S(1)} %get-tuple-element.85), channel_id=1, source_target_pairs={{0,3},{1,2},{2,1},{3,0},{4,7},{5,6},{6,5},{7,4},{8,11},{9,10},{10,... | collective-permute-start | bytes 786440 | tf_op jit(solution)/shard_map/ppermute | solution.py:35
  (67 other events, 588.8 us)
